TPU v7x, 32 devices: a whole 2x2x4 slice. The times are simulated.
32 devices in a mesh: ctx: 16 (over z, x, core), head: 2 (over y).
Axes of the slice: x: 2, y: 2, z: 4, core: 2. Of those that a mesh axis runs over, the one named last changes fastest.
Arguments:
- queries: bfloat16 [4096, 512], P('ctx', 'head'), parts along dimension 1, may hold values from -32 to 32
- keys: bfloat16 [4096, 256], P('ctx', 'head'), parts along dimension 1, may hold values from -16 to 16
- values: bfloat16 [4096, 256], P('ctx', 'head'), parts along dimension 1, may hold values from -6 to 6
- doc_starts: int32 [6], P('head'), parts along dimension 0, may hold values from 1 to 1536, as said below
Outputs:
- attended: bfloat16 [4096, 512], P('ctx', 'head'), parts along dimension 1
There are 2 independent parts, one for each index of `head`. A program takes and returns all parts, laid end to end along the dimension named above; each array names one. Nothing has to cross between parts.
Inputs may be any that keep to these rules, and one draw needn't show every extreme that they name: `doc_starts`: strictly rising; the fourth document starts at exactly 1536.
All inputs are finite; a program needn't handle non-finite values.
Results may differ from a plain program's by a relative error of at most 0.01.
Values may be sent and summed in bfloat16 or wider, within the bound.
No kernel may reach another device: no remote copies, remote signals or barrier semaphores. Data moves between devices by JAX's collectives and lax.ppermute only.
A program may use at most 64 MiB of HBM per device.

v0:
```python
import math

import jax
import jax.numpy as jnp
from jax import lax
from jax.sharding import PartitionSpec as P

D_HEAD = 128
Q_HEADS = 2


SCALE = 144.0 ** (-0.5)
NEGATIVE = -1e30


def doc_index(positions, doc_starts):
    return jnp.sum((positions[:, None] >= doc_starts[None, :]).astype(jnp.int32), axis=1)


def update_part(partial_value, target, key_block, block_start, doc_starts):
    query_rows, query_pos, query_doc, low_edge, high_edge = target
    key_count = key_block.shape[1]

    def attend(carried):
        row_max, row_total, weighted = carried
        key_pos = block_start + lax.iota(jnp.int32, key_count)
        key_doc = doc_index(key_pos, doc_starts)
        scores = (
            jnp.einsum("qhd,kd->hqk", query_rows, key_block[0], preferred_element_type=jnp.float32)
            * SCALE
        )
        visible = (key_pos[None, :] <= query_pos[:, None]) & (key_pos[None, :] >= low_edge)
        visible = (
            visible & (key_pos[None, :] < high_edge) & (key_doc[None, :] == query_doc[:, None])
        )
        scores = jnp.where(visible[None], scores, NEGATIVE)
        new_max = jnp.maximum(row_max, jnp.max(scores, axis=2))
        expo = jnp.where(visible[None], jnp.exp(scores - new_max[:, :, None]), 0.0)
        rescale = jnp.exp(row_max - new_max)
        row_total = row_total * rescale + jnp.sum(expo, axis=2)
        product = jnp.einsum(
            "hqk,kd->qhd",
            expo.astype(jnp.bfloat16),
            key_block[1],
            preferred_element_type=jnp.float32,
        )
        weighted = weighted * jnp.transpose(rescale)[:, :, None] + product
        return (new_max, row_total, weighted)

    needed = (block_start < high_edge) & (block_start + key_count > low_edge)
    return lax.cond(needed, attend, lambda carried: carried, partial_value)


def shards(queries, keys, values, doc_starts):
    shard_rows = queries.shape[0]
    my_index = lax.axis_index("ctx")
    row_iota = lax.iota(jnp.int32, shard_rows)
    own_pos = my_index * shard_rows + row_iota
    own_rows = queries.reshape(shard_rows, Q_HEADS, D_HEAD)
    own_doc = doc_index(own_pos, doc_starts)
    key_values = jnp.stack([keys, values])
    fresh_partial = (
        jnp.full((Q_HEADS, shard_rows), NEGATIVE, jnp.float32),
        jnp.zeros((Q_HEADS, shard_rows), jnp.float32),
        jnp.zeros((shard_rows, Q_HEADS, D_HEAD), jnp.float32),
    )
    targets = ((own_rows, own_pos, own_doc, jnp.int32(0), (my_index + 1) * shard_rows),)
    partials = tuple((fresh_partial for target in targets))
    shard_keys = lax.all_gather(key_values, "ctx", axis=1, tiled=True)
    key_total = shard_keys.shape[1]
    block_len = shard_rows * math.gcd(key_total // shard_rows, 4)

    def block_step(block_number, running):
        key_block = lax.dynamic_slice_in_dim(shard_keys, block_number * block_len, block_len, 1)
        block_start = block_number * block_len
        return tuple(
            (
                update_part(partial_value, target, key_block, block_start, doc_starts)
                for partial_value, target in zip(running, targets)
            )
        )

    partials = lax.fori_loop(0, key_total // block_len, block_step, partials)
    result = partials[0]
    row_max, row_total, weighted = result
    attended = weighted / jnp.transpose(row_total)[:, :, None]
    return attended.reshape(shard_rows, Q_HEADS * D_HEAD).astype(jnp.bfloat16)


def solution(mesh):
    in_specs = (P("ctx", "head"), P("ctx", "head"), P("ctx", "head"), P("head"))
    out_specs = P("ctx", "head")
    return jax.shard_map(shards, mesh=mesh, in_specs=in_specs, out_specs=out_specs, check_vma=False)
```

profile of v0, /device:TPU:25, one launch (start us, length us, event | category | flops | bytes accessed | tf_op | source)
XLA Modules:
  0.0 82.6 jit_solution(9571349763180649197)
XLA Ops:
  6.5 1.5 %pad_maximum_fusion = bf16[2,256,128]{2,1,0:T(8,128)(2,1)} fusion(bf16[1,256,128]{2,1,0:T(8,128)(2,1)} %bitcast.39, bf16[1,256,128]{2,1,0:T(8,128)(2,1)} %bitcast.40), kind=kLoop, calls=%fused_computation.31 | loop fusion | flops 65536 | bytes 262144 | tf_op jit(solution)/shard_map/stack | solution.py:61
  8.1 0.0 all-gather.2.cloned.1.call-update
  8.1 1.0 %copy.12 = bf16[256,256]{0,1:T(8,128)(2,1)S(1)} copy(bf16[256,256]{1,0:T(8,128)(2,1)} %param.8) | data formatting | bytes 262144 | tf_op args[0]
  9.1 0.1 copy.13
  9.3 0.7 convert_reduce_fusion.1
  10.0 41.2 %all-gather.2.cloned.1.call-done = bf16[2,4096,128]{2,1,0:T(8,128)(2,1)} async-done(((bf16[2,256,128]{2,1,0:T(8,128)(2,1)}), bf16[2,4096,128]{2,1,0:T(8,128)(2,1)}) %all-gather.2.cloned.1.call-update) | async-done | bytes 2097168 | tf_op jit(solution)/shard_map/all_gather | solution.py:69
  51.2 23.7 %while.18 = (s32[]{:T(128)}, f32[2,256]{1,0:T(2,128)S(1)}, f32[2,256]{1,0:T(2,128)S(1)}, f32[256,2,128]{2,0,1:T(8,128)S(1)}, s32[]{:T(128)}, /*index=5*/s32[3]{0...) while((s32[]{:T(128)}, f32[2,256]{1,0:T(2,128)S(1)}, ...), condition=%wide.region_7.8_spmd.clone, body=%wide.region_1.7_spmd.clone.sunk | while | flops 276707072 | bytes 8582549 | solution.py:83
  51.3 5.9 %conditional.3 = ((f32[2,256]{1,0:T(2,128)S(1)}, f32[2,256]{1,0:T(2,128)S(1)}, f32[256,2,128]{2,0,1:T(8,128)S(1)})) conditional(s32[]{:T(128)} %convert_element_type.37, (f32[2,256]{1,0:T(2,128)S(1)}, f32[2,256]{1,0:T(2,128)S(1)}, f32[256,2,128]{2,0,1:T(8,128)S(1)}) %tuple.50, (s32[]{:T(128)}, s32[]{:T(128)}, s32[]{:T(128)}, s32[3]{0:T(128)}, ...), branch_computations={%region_2.0_spmd, %region_3.6_spmd} | conditional | flops 276707072 | bytes 8581238 | solution.py:51
  51.3 0.7 convert_reduce_fusion
  52.1 1.2 %compare_and_fusion = pred[256,1024]{0,1:T(8,128)(4,1)S(1)} fusion(s32[256]{0:T(256)S(1)} %get-tuple-element.237, s32[256]{0:T(256)S(1)} %broadcast_add_fusion, s32[1024]{0:T(1024)S(1)} %convert_reduce_fusion, s32[1024]{0:T(1024)S(1)} %iota_add_fusion, pred[1024]{0:T(1024)(128)(4,1)S(1)} %get-tuple-element.333, pred[1024]{0:T(1024)(128)(4,1)S(1)} %get-tuple-element.334), kind=kLoop, calls=%fused_computation.12 | loop fusion | flops 1310720 | bytes 274432 | tf_op jit(solution)/shard_map/while/body/eval_jaxpr/cond/branch_1_fun/and | solution.py:34
  53.3 1.4 %fusion.2 = (f32[2,256]{1,0:T(2,128)S(1)}, f32[1024,256,2]{1,0,2:T(8,128)S(1)}) fusion(pred[256,1024]{0,1:T(8,128)(4,1)S(1)} %compare_and_fusion, bf16[256,2,128]{2,0,1:T(8,128)(2,1)S(1)} %get-tuple-element.239, bf16[2,4096,128]{2,1,0:T(8,128)(2,1)} %get-tuple-element.238, s32[]{:T(128)S(6)} %select_n.15), kind=kOutput, calls=%fused_computation.3 | convolution fusion | flops 135790080 | bytes 2754564 | tf_op jit(solution)/shard_map/while/body/eval_jaxpr/cond/branch_1_fun/qhd,kd->hqk/dot_general | solution.py:29
  54.7 1.8 %fusion.5 = f32[256,2,128]{2,0,1:T(8,128)S(1)} fusion(f32[1024,256,2]{1,0,2:T(8,128)S(1)} %get-tuple-element.332, f32[2,256]{1,0:T(2,128)S(1)} %get-tuple-element.405, pred[256,1024]{0,1:T(8,128)(4,1)S(1)} %compare_and_fusion, bf16[2,4096,128]{2,1,0:T(8,128)(2,1)} %get-tuple-element.238, s32[]{:T(128)S(6)} %add.90, s32[]{:T(128)S(6)} %select_n.15, ...), kind=kOutput, calls=%fused_computation.7 | convolution fusion | flops 136970240 | bytes 3149832 | tf_op jit(solution)/shard_map/while/body/eval_jaxpr/cond/branch_1_fun/hqk,kd->qhd/dot_general | solution.py:41
  56.6 0.6 fusion.4
  57.2 5.9 %conditional.3 = ((f32[2,256]{1,0:T(2,128)S(1)}, f32[2,256]{1,0:T(2,128)S(1)}, f32[256,2,128]{2,0,1:T(8,128)S(1)})) conditional(s32[]{:T(128)} %convert_element_type.37, (f32[2,256]{1,0:T(2,128)S(1)}, f32[2,256]{1,0:T(2,128)S(1)}, f32[256,2,128]{2,0,1:T(8,128)S(1)}) %tuple.50, (s32[]{:T(128)}, s32[]{:T(128)}, s32[]{:T(128)}, s32[3]{0:T(128)}, ...), branch_computations={%region_2.0_spmd, %region_3.6_spmd} | conditional | flops 276707072 | bytes 8581238 | solution.py:51
  57.3 0.7 convert_reduce_fusion
  58.0 1.2 %compare_and_fusion = pred[256,1024]{0,1:T(8,128)(4,1)S(1)} fusion(s32[256]{0:T(256)S(1)} %get-tuple-element.237, s32[256]{0:T(256)S(1)} %broadcast_add_fusion, s32[1024]{0:T(1024)S(1)} %convert_reduce_fusion, s32[1024]{0:T(1024)S(1)} %iota_add_fusion, pred[1024]{0:T(1024)(128)(4,1)S(1)} %get-tuple-element.333, pred[1024]{0:T(1024)(128)(4,1)S(1)} %get-tuple-element.334), kind=kLoop, calls=%fused_computation.12 | loop fusion | flops 1310720 | bytes 274432 | tf_op jit(solution)/shard_map/while/body/eval_jaxpr/cond/branch_1_fun/and | solution.py:34
  59.2 1.4 %fusion.2 = (f32[2,256]{1,0:T(2,128)S(1)}, f32[1024,256,2]{1,0,2:T(8,128)S(1)}) fusion(pred[256,1024]{0,1:T(8,128)(4,1)S(1)} %compare_and_fusion, bf16[256,2,128]{2,0,1:T(8,128)(2,1)S(1)} %get-tuple-element.239, bf16[2,4096,128]{2,1,0:T(8,128)(2,1)} %get-tuple-element.238, s32[]{:T(128)S(6)} %select_n.15), kind=kOutput, calls=%fused_computation.3 | convolution fusion | flops 135790080 | bytes 2754564 | tf_op jit(solution)/shard_map/while/body/eval_jaxpr/cond/branch_1_fun/qhd,kd->hqk/dot_general | solution.py:29
  60.6 1.8 %fusion.5 = f32[256,2,128]{2,0,1:T(8,128)S(1)} fusion(f32[1024,256,2]{1,0,2:T(8,128)S(1)} %get-tuple-element.332, f32[2,256]{1,0:T(2,128)S(1)} %get-tuple-element.405, pred[256,1024]{0,1:T(8,128)(4,1)S(1)} %compare_and_fusion, bf16[2,4096,128]{2,1,0:T(8,128)(2,1)} %get-tuple-element.238, s32[]{:T(128)S(6)} %add.90, s32[]{:T(128)S(6)} %select_n.15, ...), kind=kOutput, calls=%fused_computation.7 | convolution fusion | flops 136970240 | bytes 3149832 | tf_op jit(solution)/shard_map/while/body/eval_jaxpr/cond/branch_1_fun/hqk,kd->qhd/dot_general | solution.py:41
  62.5 0.6 fusion.4
  63.1 5.9 %conditional.3 = ((f32[2,256]{1,0:T(2,128)S(1)}, f32[2,256]{1,0:T(2,128)S(1)}, f32[256,2,128]{2,0,1:T(8,128)S(1)})) conditional(s32[]{:T(128)} %convert_element_type.37, (f32[2,256]{1,0:T(2,128)S(1)}, f32[2,256]{1,0:T(2,128)S(1)}, f32[256,2,128]{2,0,1:T(8,128)S(1)}) %tuple.50, (s32[]{:T(128)}, s32[]{:T(128)}, s32[]{:T(128)}, s32[3]{0:T(128)}, ...), branch_computations={%region_2.0_spmd, %region_3.6_spmd} | conditional | flops 276707072 | bytes 8581238 | solution.py:51
  63.2 0.7 convert_reduce_fusion
  63.9 1.2 %compare_and_fusion = pred[256,1024]{0,1:T(8,128)(4,1)S(1)} fusion(s32[256]{0:T(256)S(1)} %get-tuple-element.237, s32[256]{0:T(256)S(1)} %broadcast_add_fusion, s32[1024]{0:T(1024)S(1)} %convert_reduce_fusion, s32[1024]{0:T(1024)S(1)} %iota_add_fusion, pred[1024]{0:T(1024)(128)(4,1)S(1)} %get-tuple-element.333, pred[1024]{0:T(1024)(128)(4,1)S(1)} %get-tuple-element.334), kind=kLoop, calls=%fused_computation.12 | loop fusion | flops 1310720 | bytes 274432 | tf_op jit(solution)/shard_map/while/body/eval_jaxpr/cond/branch_1_fun/and | solution.py:34
  65.1 1.4 %fusion.2 = (f32[2,256]{1,0:T(2,128)S(1)}, f32[1024,256,2]{1,0,2:T(8,128)S(1)}) fusion(pred[256,1024]{0,1:T(8,128)(4,1)S(1)} %compare_and_fusion, bf16[256,2,128]{2,0,1:T(8,128)(2,1)S(1)} %get-tuple-element.239, bf16[2,4096,128]{2,1,0:T(8,128)(2,1)} %get-tuple-element.238, s32[]{:T(128)S(6)} %select_n.15), kind=kOutput, calls=%fused_computation.3 | convolution fusion | flops 135790080 | bytes 2754564 | tf_op jit(solution)/shard_map/while/body/eval_jaxpr/cond/branch_1_fun/qhd,kd->hqk/dot_general | solution.py:29
  66.6 1.8 %fusion.5 = f32[256,2,128]{2,0,1:T(8,128)S(1)} fusion(f32[1024,256,2]{1,0,2:T(8,128)S(1)} %get-tuple-element.332, f32[2,256]{1,0:T(2,128)S(1)} %get-tuple-element.405, pred[256,1024]{0,1:T(8,128)(4,1)S(1)} %compare_and_fusion, bf16[2,4096,128]{2,1,0:T(8,128)(2,1)} %get-tuple-element.238, s32[]{:T(128)S(6)} %add.90, s32[]{:T(128)S(6)} %select_n.15, ...), kind=kOutput, calls=%fused_computation.7 | convolution fusion | flops 136970240 | bytes 3149832 | tf_op jit(solution)/shard_map/while/body/eval_jaxpr/cond/branch_1_fun/hqk,kd->qhd/dot_general | solution.py:41
  68.4 0.6 fusion.4
  69.0 5.9 %conditional.3 = ((f32[2,256]{1,0:T(2,128)S(1)}, f32[2,256]{1,0:T(2,128)S(1)}, f32[256,2,128]{2,0,1:T(8,128)S(1)})) conditional(s32[]{:T(128)} %convert_element_type.37, (f32[2,256]{1,0:T(2,128)S(1)}, f32[2,256]{1,0:T(2,128)S(1)}, f32[256,2,128]{2,0,1:T(8,128)S(1)}) %tuple.50, (s32[]{:T(128)}, s32[]{:T(128)}, s32[]{:T(128)}, s32[3]{0:T(128)}, ...), branch_computations={%region_2.0_spmd, %region_3.6_spmd} | conditional | flops 276707072 | bytes 8581238 | solution.py:51
  69.1 0.7 convert_reduce_fusion
  69.9 1.2 %compare_and_fusion = pred[256,1024]{0,1:T(8,128)(4,1)S(1)} fusion(s32[256]{0:T(256)S(1)} %get-tuple-element.237, s32[256]{0:T(256)S(1)} %broadcast_add_fusion, s32[1024]{0:T(1024)S(1)} %convert_reduce_fusion, s32[1024]{0:T(1024)S(1)} %iota_add_fusion, pred[1024]{0:T(1024)(128)(4,1)S(1)} %get-tuple-element.333, pred[1024]{0:T(1024)(128)(4,1)S(1)} %get-tuple-element.334), kind=kLoop, calls=%fused_computation.12 | loop fusion | flops 1310720 | bytes 274432 | tf_op jit(solution)/shard_map/while/body/eval_jaxpr/cond/branch_1_fun/and | solution.py:34
  71.1 1.4 %fusion.2 = (f32[2,256]{1,0:T(2,128)S(1)}, f32[1024,256,2]{1,0,2:T(8,128)S(1)}) fusion(pred[256,1024]{0,1:T(8,128)(4,1)S(1)} %compare_and_fusion, bf16[256,2,128]{2,0,1:T(8,128)(2,1)S(1)} %get-tuple-element.239, bf16[2,4096,128]{2,1,0:T(8,128)(2,1)} %get-tuple-element.238, s32[]{:T(128)S(6)} %select_n.15), kind=kOutput, calls=%fused_computation.3 | convolution fusion | flops 135790080 | bytes 2754564 | tf_op jit(solution)/shard_map/while/body/eval_jaxpr/cond/branch_1_fun/qhd,kd->hqk/dot_general | solution.py:29
  72.5 1.8 %fusion.5 = f32[256,2,128]{2,0,1:T(8,128)S(1)} fusion(f32[1024,256,2]{1,0,2:T(8,128)S(1)} %get-tuple-element.332, f32[2,256]{1,0:T(2,128)S(1)} %get-tuple-element.405, pred[256,1024]{0,1:T(8,128)(4,1)S(1)} %compare_and_fusion, bf16[2,4096,128]{2,1,0:T(8,128)(2,1)} %get-tuple-element.238, s32[]{:T(128)S(6)} %add.90, s32[]{:T(128)S(6)} %select_n.15, ...), kind=kOutput, calls=%fused_computation.7 | convolution fusion | flops 136970240 | bytes 3149832 | tf_op jit(solution)/shard_map/while/body/eval_jaxpr/cond/branch_1_fun/hqk,kd->qhd/dot_general | solution.py:41
  74.3 0.6 fusion.4
  74.9 0.8 copy_bitcast_fusion
  (33 shorter events, 0.2 us)
Async XLA Ops:
  6.5 44.7 %all-gather.2.cloned.1.call-start = ((), (), s32[]{:S(2)}) async-start(), calls=%async_computation | async-start | bytes 2228224 | tf_op jit(solution)/shard_map/all_gather | solution.py:69
Sparse Core Ops, SparseCore 0:
  9.6 41.5 all-gather.1
where the time goes:
time: 83 us; the launch traced here: 82.6 us
  waiting for transfers between devices  41.2 us (50%)
  between operations  13.4 us (16%)
  other arithmetic  13.3 us (16%)
  matrix products  13 us (16%)
  local copies, waits for them, and re-layouts  1.17 us (1%)
    all_gather x1, waiting for transfers between devices, shards(): shard_keys = lax.all_gather(key_values, 'ctx', axis=1, tiled=True)  41.2 us
    dot_general x4, matrix products, attend(): jnp.einsum('hqk,kd->qhd', expo.astype(jnp.bfloat16), key_block[1], prefer...  7.37 us
    dot_general x4, matrix products, attend(): jnp.einsum('qhd,kd->hqk', query_rows, key_block[0], preferred_element_typ...  5.64 us
    and x4, other arithmetic, attend(): visible & (key_pos[None, :] < high_edge)  4.79 us
    reduce_sum x5, other arithmetic, doc_index(): jnp.sum((positions[:, None] >= doc_starts[None, :]).astype(jnp.int32), ax...  3.7 us
    reduce_sum x4, other arithmetic, attend(): row_total = row_total * rescale + jnp.sum(expo, axis=2)  2.26 us
  transfers between devices with their start and end apart: 1, of which 1 were waited for; matrix products, arithmetic and copies ran while one was open for 2% of the time, Pallas kernels for 0%

commit v1 on v0

v1 whole, which is shorter than its diff:
```python
import functools
import math

import jax
import jax.numpy as jnp
from jax import lax
from jax.experimental import pallas as pl
from jax.experimental.pallas import tpu as pltpu
from jax.sharding import PartitionSpec as P

D_HEAD = 128
Q_HEADS = 2
CORES = 2
SCALE = 144.0 ** (-0.5)
FACTOR = SCALE * math.log2(math.e)
MASKED = -1e30
FLOOR = -1e29
NT = (((1,), (1,)), ((), ()))


def chip_groups(chips):
    if chips % 8 == 0:
        edge = 3 * chips // 8
        return ((0, edge), (edge, chips))
    return ((0, chips),)


def rotations(chips):
    groups = chip_groups(chips)
    steps = max(high - low for low, high in groups) - 1
    plan = []
    for step in range(steps, 0, -1):
        targets = [0] * chips
        for low, high in groups:
            size = high - low
            turn = step if step < size else 1 + step % (size - 1)
            for chip in range(low, high):
                targets[chip] = low + (chip - low + turn) % size
        plan.append(targets)
    return plan


def over_cores(targets):
    return [
        (CORES * chip + core, CORES * target + core)
        for chip, target in enumerate(targets)
        for core in range(CORES)
    ]


def useful_sources(plan):
    had, tables = set(), []
    for targets in plan:
        table = [0] * len(targets)
        for chip, target in enumerate(targets):
            table[target] = target if (chip, target) in had else chip
            had.add((chip, target))
        tables.append(tuple(table))
    return tables


def pick(index, table):
    runs = [(0, table[0])]
    for place in range(1, len(table)):
        if table[place] - place != runs[-1][1] - runs[-1][0]:
            runs.append((place, table[place]))
    value = index + (runs[0][1] - runs[0][0])
    for place, entry in runs[1:]:
        value = jnp.where(index >= place, index + (entry - place), value)
    return value


def attend_kernel(seen, first, last, edge, *refs):
    starts_ref, q_ref = refs[:2]
    blocks = refs[2 : 2 + 2 * len(seen)]
    rest = refs[2 + 2 * len(seen) :]
    if not first:
        rest[-4][...], rest[-3][...], rest[-2][...] = rest[0][...], rest[1][...], rest[2][...]
    outs = rest[:-4] if first else rest[3:-4]
    total, rowmax, weighted, queries = rest[-4:]
    rows = q_ref.shape[0]
    place = lax.axis_index("ctx")
    chip = place // CORES
    core = place % CORES
    queries[:rows] = q_ref[:, :D_HEAD]
    queries[rows:] = q_ref[:, D_HEAD:]
    if first:
        total[...] = jnp.zeros_like(total)
        rowmax[...] = jnp.full_like(rowmax, FLOOR)
        weighted[...] = jnp.zeros_like(weighted)
    starts = [starts_ref[i] for i in range(starts_ref.shape[0])]
    final_pos = (place + 1) * rows - 1
    final_low = jnp.int32(0)
    for start in starts:
        final_low = jnp.where(start <= final_pos, jnp.maximum(start, final_low), final_low)

    def update(parts):
        scores = []
        for block, base, masked in parts:
            s = lax.dot_general(queries[...], block[:, :D_HEAD], NT, preferred_element_type=jnp.float32)
            if masked:
                query_pos = place * rows + lax.broadcasted_iota(jnp.int32, (rows, 1), 0)
                low = jnp.zeros_like(query_pos)
                for start in starts:
                    low = jnp.where(start <= query_pos, jnp.maximum(start, low), low)
                query_pos = jnp.concatenate([query_pos] * Q_HEADS, axis=0)
                low = jnp.concatenate([low] * Q_HEADS, axis=0)
                key_pos = base + lax.broadcasted_iota(jnp.int32, (1, rows), 1)
                s = jnp.where((key_pos <= query_pos) & (key_pos >= low), s, MASKED)
            scores.append(s)
        old = rowmax[...]
        top = jnp.max(functools.reduce(jnp.maximum, scores), axis=1, keepdims=True)
        new = jnp.maximum(old, top * FACTOR)
        rescale = jnp.exp2(old - new)
        rowmax[...] = new
        wide = jnp.concatenate([new] * (rows // D_HEAD), axis=1)
        added = jnp.zeros_like(new)
        product = None
        for s, (block, _, _) in zip(scores, parts):
            expo = jnp.exp2(s * FACTOR - wide)
            for lane in range(0, rows, D_HEAD):
                added = added + expo[:, lane : lane + D_HEAD]
            term = jnp.dot(expo.astype(jnp.bfloat16), block[:, D_HEAD:], preferred_element_type=jnp.float32)
            product = term if product is None else product + term
        total[...] = total[...] * rescale + added
        weighted[...] = weighted[...] * rescale + product

    for number, sources in enumerate(seen):
        own, twin = blocks[2 * number], blocks[2 * number + 1]
        if sources is None:
            base = chip * CORES * rows
            own_base, twin_base = place * rows, (place + 1 - 2 * core) * rows

            @pl.when(core == 0)
            def _(own=own, own_base=own_base):
                update([(own, own_base, True)])

            @pl.when(core == 1)
            def _(own=own, twin=twin, own_base=own_base, twin_base=twin_base):
                update([(own, own_base, True), (twin, twin_base, True)])

            continue
        source = pick(chip, sources)
        base = source * CORES * rows
        useful = (source < chip) & ((source >= edge) | (chip < edge)) & (base + CORES * rows > 0)
        own_base = base + core * rows
        twin_base = base + (1 - core) * rows

        @pl.when(useful & (final_low <= base))
        def _(own=own, twin=twin):
            update([(own, 0, False), (twin, 0, False)])

        @pl.when(useful & (final_low > base))
        def _(own=own, twin=twin, own_base=own_base, twin_base=twin_base):
            update([(own, own_base, True), (twin, twin_base, True)])

    if last:
        row_total = jnp.sum(total[...], axis=1, keepdims=True)
        result = weighted[...] / row_total
        for head in range(Q_HEADS):
            outs[0][:, head * D_HEAD : (head + 1) * D_HEAD] = result[head * rows : (head + 1) * rows].astype(jnp.bfloat16)
    else:
        outs[0][...], outs[1][...], outs[2][...] = total[...], rowmax[...], weighted[...]


def attend(starts, queries, blocks, seen, edge, state, last):
    rows = queries.shape[0]
    vmem = pl.BlockSpec(memory_space=pltpu.VMEM)
    wide = jax.ShapeDtypeStruct((Q_HEADS * rows, D_HEAD), jnp.float32)
    first = state is None
    operands = (queries, *blocks, *(() if first else state))
    flops = len(blocks) * Q_HEADS * rows * rows * D_HEAD * 4
    return pl.pallas_call(
        functools.partial(attend_kernel, seen, first, last, edge),
        out_shape=jax.ShapeDtypeStruct(queries.shape, jnp.bfloat16) if last else (wide,) * 3,
        in_specs=[pl.BlockSpec(memory_space=pltpu.SMEM)] + [vmem] * len(operands),
        out_specs=vmem if last else (vmem,) * 3,
        scratch_shapes=[pltpu.VMEM(wide.shape, wide.dtype)] * 3 + [pltpu.VMEM(wide.shape, jnp.bfloat16)],
        compiler_params=pltpu.CompilerParams(vmem_limit_bytes=32 * 1024 * 1024),
        cost_estimate=pl.CostEstimate(flops=flops, bytes_accessed=0, transcendentals=0),
    )(starts, *operands)


def shards(count, queries, keys, values, doc_starts):
    chips = count // CORES
    plan = rotations(chips)
    edge = chip_groups(chips)[-1][0]
    swap = [(place, place + 1 - 2 * (place % CORES)) for place in range(count)]
    own = jnp.concatenate([keys, values], axis=1)
    arrived = [lax.ppermute(own, "ctx", over_cores(targets)) for targets in plan]
    twins = [lax.ppermute(block, "ctx", swap) for block in [own, *arrived]]
    pairs = list(zip([own, *arrived], twins))
    seen = [None] + useful_sources(plan)
    state = None
    cuts = [0, 3] + list(range(5, len(pairs), 4)) + [len(pairs)] if len(pairs) > 5 else [0, 3, len(pairs)]
    for low, high in zip(cuts, cuts[1:]):
        blocks = [block for pair in pairs[low:high] for block in pair]
        state = attend(doc_starts, queries, blocks, seen[low:high], edge, state, high == len(pairs))
    return state


def solution(mesh):
    return jax.shard_map(
        functools.partial(shards, mesh.shape["ctx"]),
        mesh=mesh,
        in_specs=(P("ctx", "head"), P("ctx", "head"), P("ctx", "head"), P("head")),
        out_specs=P("ctx", "head"),
        check_vma=False,
    )
```

time: 83 us -> 21.6 us (0.26)
  the two profiles are of different devices: /device:TPU:25 before, /device:TPU:27 now
where the time goes in v1:
time: 21.6 us; the launch traced here: 21.5 us
  starting transfers between devices  11.2 us (52%)
  Pallas kernels  5.19 us (24%)
  waiting for transfers between devices  4.11 us (19%)
  local copies, waits for them, and re-layouts  0.92 us (4%)
    ppermute x5, starting transfers between devices, shards(): twins = [lax.ppermute(block, 'ctx', swap) for block in [own, *arrived]]  7.32 us
    pallas_call x2, Pallas kernels, attend(): pl.pallas_call(functools.partial(attend_kernel, seen, first, last, edge),...  5.19 us
    ppermute x4, waiting for transfers between devices, shards(): lax.ppermute(own, 'ctx', over_cores(targets))  4.1 us
    ppermute x4, starting transfers between devices, shards(): lax.ppermute(own, 'ctx', over_cores(targets))  3.88 us
    unnamed x7, local copies, waits for them, and re-layouts  0.9 us
  transfers between devices with their start and end apart: 9, of which 2 were waited for; matrix products, arithmetic and copies ran while one was open for 0% of the time, Pallas kernels for 12%

profile of v1, /device:TPU:27, one launch (start us, length us, event | category | flops | bytes accessed | tf_op | source)
XLA Modules:
  0.0 21.5 jit_solution(4171597670650527274)
XLA Ops:
  0.0 0.0 copy-start.2
  0.0 0.0 copy-start
  0.0 0.9 %constant_dynamic-update-slice_fusion.1 = bf16[256,256]{1,0:T(8,128)(2,1)S(1)} fusion(bf16[256,128]{1,0:T(8,128)(2,1)} %param.5), kind=kLoop, calls=%fused_computation.1 | loop fusion | bytes 131072
  0.9 0.0 copy-done.2
  0.9 0.0 copy-start.1
  0.9 0.2 %collective-permute-start.7 = (bf16[256,256]{1,0:T(8,128)(2,1)S(1)}, bf16[256,256]{1,0:T(8,128)(2,1)S(1)}, u32[]{:S(2)}, u32[]{:S(2)}) collective-permute-start(bf16[256,256]{1,0:T(8,128)(2,1)S(1)} %constant_dynamic-update-slice_fusion.refs_2_), channel_id=1, source_target_pairs={{0,8},{2,10},{4,0},{6,2},{8,4},{10,6},{12,24},{14,26},{16,28},{18,... | collective-permute-start | bytes 393224 | tf_op jit(solution)/shard_map/ppermute | solution.py:190
  1.2 0.3 %collective-permute-start.5 = (bf16[256,256]{1,0:T(8,128)(2,1)S(1)}, bf16[256,256]{1,0:T(8,128)(2,1)S(1)}, u32[]{:S(2)}, u32[]{:S(2)}) collective-permute-start(bf16[256,256]{1,0:T(8,128)(2,1)S(1)} %constant_dynamic-update-slice_fusion.refs_2_), channel_id=1, source_target_pairs={{0,4},{2,6},{4,8},{6,10},{8,0},{10,2},{12,28},{14,30},{16,12},{18,... | collective-permute-start | bytes 393224 | tf_op jit(solution)/shard_map/ppermute | solution.py:190
  1.4 2.1 %collective-permute-start.2 = (bf16[256,256]{1,0:T(8,128)(2,1)S(1)}, bf16[256,256]{1,0:T(8,128)(2,1)S(1)}, u32[]{:S(2)}, u32[]{:S(2)}) collective-permute-start(bf16[256,256]{1,0:T(8,128)(2,1)S(1)} %constant_dynamic-update-slice_fusion.refs_2_), channel_id=1, source_target_pairs={{0,4},{2,6},{4,8},{6,10},{8,0},{10,2},{12,16},{14,18},{16,20},{18,... | collective-permute-start | bytes 393224 | tf_op jit(solution)/shard_map/ppermute | solution.py:190
  3.5 1.3 %collective-permute-start = (bf16[256,256]{1,0:T(8,128)(2,1)S(1)}, bf16[256,256]{1,0:T(8,128)(2,1)S(1)}, u32[]{:S(2)}, u32[]{:S(2)}) collective-permute-start(bf16[256,256]{1,0:T(8,128)(2,1)S(1)} %constant_dynamic-update-slice_fusion.refs_2_), channel_id=1, source_target_pairs={{0,8},{2,10},{4,0},{6,2},{8,4},{10,6},{12,20},{14,22},{16,24},{18,... | collective-permute-start | bytes 393224 | tf_op jit(solution)/shard_map/ppermute | solution.py:190
  4.8 1.8 %collective-permute-start.4 = (bf16[256,256]{1,0:T(8,128)(2,1)S(1)}, bf16[256,256]{1,0:T(8,128)(2,1)S(1)}, u32[]{:S(2)}, u32[]{:S(2)}) collective-permute-start(bf16[256,256]{1,0:T(8,128)(2,1)S(1)} %constant_dynamic-update-slice_fusion.refs_2_), channel_id=1, source_target_pairs={{0,2},{2,0},{4,6},{6,4},{8,10},{10,8},{12,14},{14,12},{16,18},{18,... | collective-permute-start | bytes 393224 | tf_op jit(solution)/shard_map/ppermute | solution.py:191
  6.6 0.0 collective-permute-done.7.refs_6_
  6.6 2.3 %collective-permute-start.8 = (bf16[256,256]{1,0:T(8,128)(2,1)S(1)}, bf16[256,256]{1,0:T(8,128)(2,1)S(1)}, u32[]{:S(2)}, u32[]{:S(2)}) collective-permute-start(bf16[256,256]{1,0:T(8,128)(2,1)S(1)} %collective-permute-done.7.refs_6_), channel_id=1, source_target_pairs={{0,2},{2,0},{4,6},{6,4},{8,10},{10,8},{12,14},{14,12},{16,18},{18,... | collective-permute-start | bytes 393224 | tf_op jit(solution)/shard_map/ppermute | solution.py:191
  9.0 0.2 collective-permute-done.5.refs_4_
  9.1 2.7 %collective-permute-start.6 = (bf16[256,256]{1,0:T(8,128)(2,1)S(1)}, bf16[256,256]{1,0:T(8,128)(2,1)S(1)}, u32[]{:S(2)}, u32[]{:S(2)}) collective-permute-start(bf16[256,256]{1,0:T(8,128)(2,1)S(1)} %collective-permute-done.5.refs_4_), channel_id=1, source_target_pairs={{0,2},{2,0},{4,6},{6,4},{8,10},{10,8},{12,14},{14,12},{16,18},{18,... | collective-permute-start | bytes 393224 | tf_op jit(solution)/shard_map/ppermute | solution.py:191
  11.8 0.0 collective-permute-done.2.refs_4_
  11.8 0.0 collective-permute-start.3
  11.8 3.9 %collective-permute-done.refs_2_ = bf16[256,256]{1,0:T(8,128)(2,1)S(1)} collective-permute-done((bf16[256,256]{1,0:T(8,128)(2,1)S(1)}, bf16[256,256]{1,0:T(8,128)(2,1)S(1)}, u32[]{:S(2)}, u32[]{:S(2)}) %collective-permute-start) | collective-permute-done | bytes 131104 | tf_op jit(solution)/shard_map/ppermute | solution.py:190
  15.8 0.5 %collective-permute-start.1 = (bf16[256,256]{1,0:T(8,128)(2,1)S(1)}, bf16[256,256]{1,0:T(8,128)(2,1)S(1)}, u32[]{:S(2)}, u32[]{:S(2)}) collective-permute-start(bf16[256,256]{1,0:T(8,128)(2,1)S(1)} %collective-permute-done.refs_2_), channel_id=1, source_target_pairs={{0,2},{2,0},{4,6},{6,4},{8,10},{10,8},{12,14},{14,12},{16,18},{18,... | collective-permute-start | bytes 393224 | tf_op jit(solution)/shard_map/ppermute | solution.py:191
  16.3 0.0 collective-permute-done.4.refs_3_
  16.3 0.0 collective-permute-done.8.refs_7_
  16.3 0.0 collective-permute-done.6.refs_5_
  16.3 0.0 copy-done
  16.3 0.0 copy-done.1
  16.3 2.6 %shard_map.46 = (f32[512,128]{1,0:T(8,128)S(1)}, f32[512,128]{1,0:T(8,128)S(1)}, f32[512,128]{1,0:T(8,128)S(1)}) custom-call(s32[3]{0:T(128)S(1)} %copy-done.1, bf16[256,256]{1,0:T(8,128)(2,1)S(1)} %copy-done, bf16[256,256]{1,0:T(8,128)(2,1)S(1)} %constant_dynamic-update-slice_fusion.refs_2_, bf16[256,256]{1,0:T(8,128)(2,1)S(1)} %collective-permute-done.4.refs_3_, ...), custom_call_target="tpu_custom_call" | custom-call | flops 402653184 | tf_op jit(solution)/shard_map/pallas_call | solution.py:173
  18.9 0.0 collective-permute-done.3.refs_5_
  18.9 0.0 collective-permute-done.1.refs_3_
  18.9 2.6 %shard_map.47 = bf16[256,256]{1,0:T(8,128)(2,1)} custom-call(s32[3]{0:T(128)S(1)} %copy-done.1, bf16[256,256]{1,0:T(8,128)(2,1)S(1)} %copy-done, bf16[256,256]{1,0:T(8,128)(2,1)S(1)} %collective-permute-done.refs_2_, bf16[256,256]{1,0:T(8,128)(2,1)S(1)} %collective-permute-done.1.refs_3_, bf16[256,256]{1,0:T(8,128)(2,1)S(1)} %collective-permute-done.2.refs_4_, ...), custom_call_target="tpu_custom_call" | custom-call | flops 268435456 | tf_op jit(solution)/shard_map/pallas_call | solution.py:173
  (1 shorter events, 0.0 us)
Async XLA Ops:
  0.0 0.9 %copy-start.2 = (bf16[256,128]{1,0:T(8,128)(2,1)S(1)}, bf16[256,128]{1,0:T(8,128)(2,1)}, u32[]{:S(2)}) copy-start(bf16[256,128]{1,0:T(8,128)(2,1)} %param.6) | copy-start | bytes 196612
  0.0 16.3 %copy-start = (bf16[256,256]{1,0:T(8,128)(2,1)S(1)}, bf16[256,256]{1,0:T(8,128)(2,1)}, u32[]{:S(2)}) copy-start(bf16[256,256]{1,0:T(8,128)(2,1)} %refs_1_.3) | copy-start | bytes 393220
  0.9 15.4 %copy-start.1 = (s32[3]{0:T(128)S(1)}, s32[3]{0:T(128)}, u32[]{:S(2)}) copy-start(s32[3]{0:T(128)} %refs_0_.3) | copy-start | bytes 40
  0.9 5.7 %collective-permute-start.7 = (bf16[256,256]{1,0:T(8,128)(2,1)S(1)}, bf16[256,256]{1,0:T(8,128)(2,1)S(1)}, u32[]{:S(2)}, u32[]{:S(2)}) collective-permute-start(bf16[256,256]{1,0:T(8,128)(2,1)S(1)} %constant_dynamic-update-slice_fusion.refs_2_), channel_id=1, source_target_pairs={{0,8},{2,10},{4,0},{6,2},{8,4},{10,6},{12,24},{14,26},{16,28},{18,... | collective-permute-start | bytes 393224 | tf_op jit(solution)/shard_map/ppermute | solution.py:190
  1.2 8.0 %collective-permute-start.5 = (bf16[256,256]{1,0:T(8,128)(2,1)S(1)}, bf16[256,256]{1,0:T(8,128)(2,1)S(1)}, u32[]{:S(2)}, u32[]{:S(2)}) collective-permute-start(bf16[256,256]{1,0:T(8,128)(2,1)S(1)} %constant_dynamic-update-slice_fusion.refs_2_), channel_id=1, source_target_pairs={{0,4},{2,6},{4,8},{6,10},{8,0},{10,2},{12,28},{14,30},{16,12},{18,... | collective-permute-start | bytes 393224 | tf_op jit(solution)/shard_map/ppermute | solution.py:190
  1.4 10.4 %collective-permute-start.2 = (bf16[256,256]{1,0:T(8,128)(2,1)S(1)}, bf16[256,256]{1,0:T(8,128)(2,1)S(1)}, u32[]{:S(2)}, u32[]{:S(2)}) collective-permute-start(bf16[256,256]{1,0:T(8,128)(2,1)S(1)} %constant_dynamic-update-slice_fusion.refs_2_), channel_id=1, source_target_pairs={{0,4},{2,6},{4,8},{6,10},{8,0},{10,2},{12,16},{14,18},{16,20},{18,... | collective-permute-start | bytes 393224 | tf_op jit(solution)/shard_map/ppermute | solution.py:190
  3.5 12.2 %collective-permute-start = (bf16[256,256]{1,0:T(8,128)(2,1)S(1)}, bf16[256,256]{1,0:T(8,128)(2,1)S(1)}, u32[]{:S(2)}, u32[]{:S(2)}) collective-permute-start(bf16[256,256]{1,0:T(8,128)(2,1)S(1)} %constant_dynamic-update-slice_fusion.refs_2_), channel_id=1, source_target_pairs={{0,8},{2,10},{4,0},{6,2},{8,4},{10,6},{12,20},{14,22},{16,24},{18,... | collective-permute-start | bytes 393224 | tf_op jit(solution)/shard_map/ppermute | solution.py:190
  4.8 11.4 %collective-permute-start.4 = (bf16[256,256]{1,0:T(8,128)(2,1)S(1)}, bf16[256,256]{1,0:T(8,128)(2,1)S(1)}, u32[]{:S(2)}, u32[]{:S(2)}) collective-permute-start(bf16[256,256]{1,0:T(8,128)(2,1)S(1)} %constant_dynamic-update-slice_fusion.refs_2_), channel_id=1, source_target_pairs={{0,2},{2,0},{4,6},{6,4},{8,10},{10,8},{12,14},{14,12},{16,18},{18,... | collective-permute-start | bytes 393224 | tf_op jit(solution)/shard_map/ppermute | solution.py:191
  6.6 9.6 %collective-permute-start.8 = (bf16[256,256]{1,0:T(8,128)(2,1)S(1)}, bf16[256,256]{1,0:T(8,128)(2,1)S(1)}, u32[]{:S(2)}, u32[]{:S(2)}) collective-permute-start(bf16[256,256]{1,0:T(8,128)(2,1)S(1)} %collective-permute-done.7.refs_6_), channel_id=1, source_target_pairs={{0,2},{2,0},{4,6},{6,4},{8,10},{10,8},{12,14},{14,12},{16,18},{18,... | collective-permute-start | bytes 393224 | tf_op jit(solution)/shard_map/ppermute | solution.py:191
  9.1 7.1 %collective-permute-start.6 = (bf16[256,256]{1,0:T(8,128)(2,1)S(1)}, bf16[256,256]{1,0:T(8,128)(2,1)S(1)}, u32[]{:S(2)}, u32[]{:S(2)}) collective-permute-start(bf16[256,256]{1,0:T(8,128)(2,1)S(1)} %collective-permute-done.5.refs_4_), channel_id=1, source_target_pairs={{0,2},{2,0},{4,6},{6,4},{8,10},{10,8},{12,14},{14,12},{16,18},{18,... | collective-permute-start | bytes 393224 | tf_op jit(solution)/shard_map/ppermute | solution.py:191
  11.8 7.0 %collective-permute-start.3 = (bf16[256,256]{1,0:T(8,128)(2,1)S(1)}, bf16[256,256]{1,0:T(8,128)(2,1)S(1)}, u32[]{:S(2)}, u32[]{:S(2)}) collective-permute-start(bf16[256,256]{1,0:T(8,128)(2,1)S(1)} %collective-permute-done.2.refs_4_), channel_id=1, source_target_pairs={{0,2},{2,0},{4,6},{6,4},{8,10},{10,8},{12,14},{14,12},{16,18},{18,... | collective-permute-start | bytes 393224 | tf_op jit(solution)/shard_map/ppermute | solution.py:191
  15.8 3.1 %collective-permute-start.1 = (bf16[256,256]{1,0:T(8,128)(2,1)S(1)}, bf16[256,256]{1,0:T(8,128)(2,1)S(1)}, u32[]{:S(2)}, u32[]{:S(2)}) collective-permute-start(bf16[256,256]{1,0:T(8,128)(2,1)S(1)} %collective-permute-done.refs_2_), channel_id=1, source_target_pairs={{0,2},{2,0},{4,6},{6,4},{8,10},{10,8},{12,14},{14,12},{16,18},{18,... | collective-permute-start | bytes 393224 | tf_op jit(solution)/shard_map/ppermute | solution.py:191

commit v2 on v1

v2 whole, which is shorter than its diff:
```python
import functools
import math

import jax
import jax.numpy as jnp
from jax import lax
from jax.experimental import pallas as pl
from jax.experimental.pallas import tpu as pltpu
from jax.sharding import PartitionSpec as P

D_HEAD = 128
Q_HEADS = 2
CORES = 2
STAT_ROWS = 8
SCALE = 144.0 ** (-0.5)
FACTOR = SCALE * math.log2(math.e)
MASKED = -1e30
FLOOR = -1e29
NT = (((1,), (1,)), ((), ()))
TN = (((0,), (0,)), ((), ()))


def chip_groups(chips):
    if chips % 8 == 0:
        edge = 3 * chips // 8
        return ((0, edge), (edge, chips))
    return ((0, chips),)


def rotations(chips):
    groups = chip_groups(chips)
    steps = max(high - low for low, high in groups) - 1
    plan = []
    for step in range(steps, 0, -1):
        targets = [0] * chips
        for low, high in groups:
            size = high - low
            turn = step if step < size else 1 + step % (size - 1)
            for chip in range(low, high):
                targets[chip] = low + (chip - low + turn) % size
        plan.append((None, targets))
    return plan


def slots_of(chips):
    N = None
    if chips == 8:
        return [
            (None, [1, 2, 0, 4, 6, 7, 3, 5]),
            (None, [2, None, 0, 7, 5, 6, 4, 3]),
            (None, [None, None, None, 5, None, 3, 7, 6]),
            (0, [None, None, None, None, 6, None, 7, 4]),
        ]
    return rotations(chips)


def stages_of(chips, count):
    if chips == 8:
        return [[0], [2], [1, 3]]
    return [list(range(low, min(low + 4, count))) for low in range(0, count, 4)]


def over_cores(targets):
    return [
        (CORES * chip + core, CORES * chip + 1 - core if target is None else CORES * target + core)
        for chip, target in enumerate(targets)
        for core in range(CORES)
    ]


def useful_sources(plan):
    had, origins, tables = set(), [], []
    for operand, targets in plan:
        origin = list(range(len(targets)))
        for chip, target in enumerate(targets):
            if target is not None:
                origin[target] = chip if operand is None else origins[operand][chip]
        origins.append(origin)
        tables.append(tuple(chip if (source, chip) in had else source for chip, source in enumerate(origin)))
        had.update((source, chip) for chip, source in enumerate(origin))
    for low, high in chip_groups(len(origins[0])):
        for chip in range(low, high):
            assert all((source, chip) in had for source in range(low, chip))
    return tables


def pick(index, table):
    runs = [(0, table[0])]
    for place in range(1, len(table)):
        if table[place] - place != runs[-1][1] - runs[-1][0]:
            runs.append((place, table[place]))
    value = index + (runs[0][1] - runs[0][0])
    for place, entry in runs[1:]:
        value = jnp.where(index >= place, index + (entry - place), value)
    return value


def attend_kernel(tables, first, edge, *refs):
    starts_ref, own_q, twin_q = refs[:3]
    count = len(tables) + (1 if first else 0)
    blocks = refs[3 : 3 + count]
    olds, news = refs[3 + count : -2], refs[-2:]
    rows = own_q.shape[0]
    place = lax.axis_index("ctx")
    chip, core = place // CORES, place % CORES
    last_group = chip >= edge
    chunks = [(which, head) for which in range(CORES) for head in range(Q_HEADS)]

    def mask_of(which, key_base):
        query_place = place if which == 0 else place + 1 - 2 * core
        query_pos = query_place * rows + lax.broadcasted_iota(jnp.int32, (1, rows), 1)
        low = jnp.zeros_like(query_pos)
        for number in range(starts_ref.shape[1]):
            start = starts_ref[:, number : number + 1]
            low = jnp.where(start <= query_pos, jnp.maximum(start, low), low)
        key_pos = key_base + lax.broadcasted_iota(jnp.int32, (rows, 1), 0)
        return (key_pos <= query_pos) & (key_pos >= low)

    def update(olds, which, head, parts):
        queries = (own_q, twin_q)[which][:, head * D_HEAD : (head + 1) * D_HEAD]
        new = news[which]
        scores = []
        for block, mask in parts:
            s = lax.dot_general(block[:, :D_HEAD], queries, NT, preferred_element_type=jnp.float32)
            scores.append(s if mask is None else jnp.where(mask, s, MASKED))
        top = functools.reduce(jnp.maximum, [jnp.max(s, axis=0, keepdims=True) for s in scores]) * FACTOR
        if olds is None:
            top = jnp.maximum(top, FLOOR)
        else:
            old = olds[which]
            old_top = old[head, D_HEAD : D_HEAD + 1]
            top = jnp.maximum(top, old_top)
        total, weighted = None, None
        for s, (block, _) in zip(scores, parts):
            expo = jnp.exp2(s * FACTOR - top)
            added = jnp.sum(expo, axis=0, keepdims=True)
            term = lax.dot_general(
                block[:, D_HEAD:], expo.astype(jnp.bfloat16), TN, preferred_element_type=jnp.float32
            )
            total = added if total is None else total + added
            weighted = term if weighted is None else weighted + term
        if olds is not None:
            rescale = jnp.exp2(old_top - top)
            total = total + old[head, D_HEAD + 1 : D_HEAD + 2] * rescale
            weighted = weighted + old[head, :D_HEAD] * rescale
        new[head, :D_HEAD] = weighted
        new[head, D_HEAD : D_HEAD + 1] = top
        new[head, D_HEAD + 1 : D_HEAD + 2] = total

    received = []
    for table, block in zip(tables, blocks[count - len(tables) :]):
        source = pick(chip, table)
        useful = (source < chip) & ((source >= edge) | (chip < edge))
        received.append((block, source, useful, any(entry < number for number, entry in enumerate(table[:edge]))))

    def one_by_one():
        for block, source, useful, early in received:

            @pl.when(useful & last_group)
            def _(block=block):
                for which, head in chunks:
                    update(news, which, head, [(block, None)])

            if early:

                @pl.when(useful & jnp.logical_not(last_group))
                def _(block=block, source=source):
                    for which in range(CORES):
                        mask = mask_of(which, (source * CORES + core) * rows)
                        for head in range(Q_HEADS):
                            update(news, which, head, [(block, mask)])

    if first:
        own_mask = mask_of(0, place * rows)
        for head in range(Q_HEADS):
            update(None, 0, head, [(blocks[0], own_mask)])

        @pl.when(core == 0)
        def _():
            mask = mask_of(1, place * rows)
            for head in range(Q_HEADS):
                update(None, 1, head, [(blocks[0], mask)])

        @pl.when(core == 1)
        def _():
            news[1][...] = jnp.zeros_like(news[1])
            news[1][:, D_HEAD : D_HEAD + 1] = jnp.full((Q_HEADS, 1, rows), FLOOR, jnp.float32)

        one_by_one()
    else:
        every = functools.reduce(jnp.logical_and, [useful for _, _, useful, _ in received], last_group)

        @pl.when(every)
        def _():
            for which, head in chunks:
                update(olds, which, head, [(block, None) for block, _, _, _ in received])

        @pl.when(jnp.logical_not(every))
        def _():
            for which in range(CORES):
                news[which][...] = olds[which][...]
            one_by_one()


def merge_kernel(own_ref, twin_ref, out_ref):
    for head in range(Q_HEADS):
        own_top, twin_top = own_ref[head, D_HEAD : D_HEAD + 1], twin_ref[head, D_HEAD : D_HEAD + 1]
        top = jnp.maximum(own_top, twin_top)
        own_scale, twin_scale = jnp.exp2(own_top - top), jnp.exp2(twin_top - top)
        total = (
            own_ref[head, D_HEAD + 1 : D_HEAD + 2] * own_scale + twin_ref[head, D_HEAD + 1 : D_HEAD + 2] * twin_scale
        )
        result = own_ref[head, :D_HEAD] * (own_scale / total) + twin_ref[head, :D_HEAD] * (twin_scale / total)
        out_ref[:, head * D_HEAD : (head + 1) * D_HEAD] = result.T.astype(jnp.bfloat16)


def vmem_call(kernel, out_shape, operands, flops):
    vmem = pl.BlockSpec(memory_space=pltpu.VMEM)
    return pl.pallas_call(
        kernel,
        out_shape=out_shape,
        in_specs=[vmem] * len(operands),
        out_specs=jax.tree.map(lambda _: vmem, out_shape),
        compiler_params=pltpu.CompilerParams(vmem_limit_bytes=32 * 1024 * 1024),
        cost_estimate=pl.CostEstimate(flops=flops, bytes_accessed=0, transcendentals=0),
    )(*operands)


def shards(count, queries, keys, values, doc_starts):
    chips = count // CORES
    plan = slots_of(chips)
    edge = chip_groups(chips)[-1][0]
    rows = queries.shape[0]
    swap = [(place, place + 1 - 2 * (place % CORES)) for place in range(count)]
    seen = useful_sources(plan)
    starts = doc_starts.reshape(1, -1)
    twin_queries = lax.ppermute(queries, "ctx", swap)
    own = jnp.concatenate([keys, values], axis=1)
    arrived = []
    for operand, targets in plan:
        block = own if operand is None else arrived[operand]
        arrived.append(lax.ppermute(block, "ctx", over_cores(targets)))
    partial = jax.ShapeDtypeStruct((Q_HEADS, D_HEAD + STAT_ROWS, rows), jnp.float32)
    state = ()
    for slots in stages_of(chips, len(plan)):
        blocks = ([] if state else [own]) + [arrived[slot] for slot in slots]
        tables = [seen[slot] for slot in slots]
        flops = len(blocks) * CORES * Q_HEADS * rows * rows * D_HEAD * 4
        kernel = functools.partial(attend_kernel, tables, not state, edge)
        state = vmem_call(kernel, (partial, partial), (starts, queries, twin_queries, *blocks, *state), flops)
    mine, others = state
    out_shape = jax.ShapeDtypeStruct(queries.shape, jnp.bfloat16)
    return vmem_call(merge_kernel, out_shape, (mine, lax.ppermute(others, "ctx", swap)), 1000)


def solution(mesh):
    return jax.shard_map(
        functools.partial(shards, mesh.shape["ctx"]),
        mesh=mesh,
        in_specs=(P("ctx", "head"), P("ctx", "head"), P("ctx", "head"), P("head")),
        out_specs=P("ctx", "head"),
        check_vma=False,
    )
```

time: 21.6 us -> 17.4 us (0.81)
  the two profiles are of different devices: /device:TPU:27 before, /device:TPU:25 now
where the time goes in v2:
time: 17.4 us; the launch traced here: 17.3 us
  starting transfers between devices  6.35 us (36%)
  waiting for transfers between devices  5.22 us (30%)
  Pallas kernels  4.72 us (27%)
  local copies, waits for them, and re-layouts  0.92 us (5%)
    pallas_call x4, Pallas kernels, vmem_call(): pl.pallas_call(kernel, out_shape=out_shape, in_specs=[vmem] * len(operand...  4.72 us
    ppermute x4, waiting for transfers between devices, shards(): arrived.append(lax.ppermute(block, 'ctx', over_cores(targets)))  4.04 us
    ppermute x4, starting transfers between devices, shards(): arrived.append(lax.ppermute(block, 'ctx', over_cores(targets)))  2.73 us
    ppermute x1, starting transfers between devices, shards(): lax.ppermute(others, 'ctx', swap)  2.67 us
    ppermute x1, waiting for transfers between devices, shards(): lax.ppermute(others, 'ctx', swap)  1.19 us
    ppermute x1, starting transfers between devices, shards(): twin_queries = lax.ppermute(queries, 'ctx', swap)  0.96 us
    unnamed x7, local copies, waits for them, and re-layouts  0.9 us
  transfers between devices with their start and end apart: 6, of which 3 were waited for; matrix products, arithmetic and copies ran while one was open for 0% of the time, Pallas kernels for 12%

profile of v2, /device:TPU:25, one launch (start us, length us, event | category | flops | bytes accessed | tf_op | source)
XLA Modules:
  0.0 17.3 jit_solution(10691198964096303913)
XLA Ops:
  0.0 0.0 copy-start.2
  0.0 0.0 copy-start
  0.0 0.9 %constant_dynamic-update-slice_fusion.1 = bf16[256,256]{1,0:T(8,128)(2,1)S(1)} fusion(bf16[256,128]{1,0:T(8,128)(2,1)} %param.5), kind=kLoop, calls=%fused_computation.1 | loop fusion | bytes 131072
  0.9 0.0 copy-done.2
  0.9 0.0 copy-start.1
  0.9 1.0 %collective-permute-start.2 = (bf16[256,256]{1,0:T(8,128)(2,1)S(1)}, bf16[256,256]{1,0:T(8,128)(2,1)S(1)}, u32[]{:S(2)}, u32[]{:S(2)}) collective-permute-start(bf16[256,256]{1,0:T(8,128)(2,1)S(1)} %constant_dynamic-update-slice_fusion.refs_3_), channel_id=1, source_target_pairs={{0,4},{2,6},{4,8},{6,10},{8,0},{10,2},{12,16},{14,18},{16,24},{18,... | collective-permute-start | bytes 393224 | tf_op jit(solution)/shard_map/ppermute | solution.py:242
  2.0 0.0 copy-done
  2.0 1.0 %collective-permute-start = (bf16[256,256]{1,0:T(8,128)(2,1)S(1)}, bf16[256,256]{1,0:T(8,128)(2,1)S(1)}, u32[]{:S(2)}, u32[]{:S(2)}) collective-permute-start(bf16[256,256]{1,0:T(8,128)(2,1)S(1)} %copy-done), channel_id=1, source_target_pairs={{0,2},{2,0},{4,6},{6,4},{8,10},{10,8},{12,14},{14,12},{16,18},{18,... | collective-permute-start | bytes 393224 | tf_op jit(solution)/shard_map/ppermute | solution.py:237
  2.9 0.4 %collective-permute-start.4 = (bf16[256,256]{1,0:T(8,128)(2,1)S(1)}, bf16[256,256]{1,0:T(8,128)(2,1)S(1)}, u32[]{:S(2)}, u32[]{:S(2)}) collective-permute-start(bf16[256,256]{1,0:T(8,128)(2,1)S(1)} %constant_dynamic-update-slice_fusion.refs_3_), channel_id=1, source_target_pairs={{0,2},{2,0},{4,6},{6,4},{8,10},{10,8},{12,20},{14,22},{16,18},{18,... | collective-permute-start | bytes 393224 | tf_op jit(solution)/shard_map/ppermute | solution.py:242
  3.3 0.1 collective-permute-start.1
  3.4 1.9 %collective-permute-done.2.refs_4_ = bf16[256,256]{1,0:T(8,128)(2,1)S(1)} collective-permute-done((bf16[256,256]{1,0:T(8,128)(2,1)S(1)}, bf16[256,256]{1,0:T(8,128)(2,1)S(1)}, u32[]{:S(2)}, u32[]{:S(2)}) %collective-permute-start.2) | collective-permute-done | bytes 131104 | tf_op jit(solution)/shard_map/ppermute | solution.py:242
  5.4 1.2 %collective-permute-start.3 = (bf16[256,256]{1,0:T(8,128)(2,1)S(1)}, bf16[256,256]{1,0:T(8,128)(2,1)S(1)}, u32[]{:S(2)}, u32[]{:S(2)}) collective-permute-start(bf16[256,256]{1,0:T(8,128)(2,1)S(1)} %collective-permute-done.2.refs_4_), channel_id=1, source_target_pairs={{0,2},{2,0},{4,6},{6,4},{8,10},{10,8},{12,14},{14,12},{16,24},{18,... | collective-permute-start | bytes 393224 | tf_op jit(solution)/shard_map/ppermute | solution.py:242
  6.6 0.0 collective-permute-done.refs_2_
  6.6 0.0 copy-done.1
  6.6 2.1 %shard_map.46 = (f32[2,136,256]{2,1,0:T(8,128)S(1)}, f32[2,136,256]{2,1,0:T(8,128)S(1)}) custom-call(s32[1,3]{1,0:T(1,128)S(1)} %bitcast.1, bf16[256,256]{1,0:T(8,128)(2,1)S(1)} %copy-done, bf16[256,256]{1,0:T(8,128)(2,1)S(1)} %collective-permute-done.refs_2_, bf16[256,256]{1,0:T(8,128)(2,1)S(1)} %constant_dynamic-update-slice_fusion.refs_3_, ...), custom_call_target="tpu_custom_call" | custom-call | flops 268435456 | tf_op jit(solution)/shard_map/pallas_call | solution.py:219
  8.7 2.1 %collective-permute-done.4.refs_3_ = bf16[256,256]{1,0:T(8,128)(2,1)S(1)} collective-permute-done((bf16[256,256]{1,0:T(8,128)(2,1)S(1)}, bf16[256,256]{1,0:T(8,128)(2,1)S(1)}, u32[]{:S(2)}, u32[]{:S(2)}) %collective-permute-start.4) | collective-permute-done | bytes 131104 | tf_op jit(solution)/shard_map/ppermute | solution.py:242
  10.8 0.0 collective-permute-done.1.refs_3_
  10.8 0.0 collective-permute-done.3.refs_4_
  10.9 1.8 %shard_map.48 = (f32[2,136,256]{2,1,0:T(8,128)S(1)}, f32[2,136,256]{2,1,0:T(8,128)S(1)}) custom-call(s32[1,3]{1,0:T(1,128)S(1)} %bitcast.3, bf16[256,256]{1,0:T(8,128)(2,1)S(1)} %copy-done, bf16[256,256]{1,0:T(8,128)(2,1)S(1)} %collective-permute-done.refs_2_, bf16[256,256]{1,0:T(8,128)(2,1)S(1)} %collective-permute-done.1.refs_3_, ...), custom_call_target="tpu_custom_call" | custom-call | flops 268435456 | tf_op jit(solution)/shard_map/pallas_call | solution.py:219
  12.7 2.7 %collective-permute-start.5 = (f32[2,136,256]{2,1,0:T(8,128)S(1)}, f32[2,136,256]{2,1,0:T(8,128)S(1)}, u32[]{:S(2)}, u32[]{:S(2)}) collective-permute-start(f32[2,136,256]{2,1,0:T(8,128)S(1)} %get-tuple-element.16), channel_id=1, source_target_pairs={{0,2},{2,0},{4,6},{6,4},{8,10},{10,8},{12,14},{14,12},{16,18},{18,... | collective-permute-start | bytes 835592 | tf_op jit(solution)/shard_map/ppermute | solution.py:253
  15.3 1.2 %collective-permute-done.5.twin_ref = f32[2,136,256]{2,1,0:T(8,128)S(1)} collective-permute-done((f32[2,136,256]{2,1,0:T(8,128)S(1)}, f32[2,136,256]{2,1,0:T(8,128)S(1)}, u32[]{:S(2)}, u32[]{:S(2)}) %collective-permute-start.5) | collective-permute-done | bytes 278560 | tf_op jit(solution)/shard_map/ppermute | solution.py:253
  16.5 0.8 %shard_map.49 = bf16[256,256]{1,0:T(8,128)(2,1)} custom-call(f32[2,136,256]{2,1,0:T(8,128)S(1)} %get-tuple-element.15.own_ref, f32[2,136,256]{2,1,0:T(8,128)S(1)} %collective-permute-done.5.twin_ref), custom_call_target="tpu_custom_call" | custom-call | flops 1000 | tf_op jit(solution)/shard_map/pallas_call | solution.py:219
  (2 shorter events, 0.1 us)
Async XLA Ops:
  0.0 0.9 %copy-start.2 = (bf16[256,128]{1,0:T(8,128)(2,1)S(1)}, bf16[256,128]{1,0:T(8,128)(2,1)}, u32[]{:S(2)}) copy-start(bf16[256,128]{1,0:T(8,128)(2,1)} %param.6) | copy-start | bytes 196612
  0.0 2.0 %copy-start = (bf16[256,256]{1,0:T(8,128)(2,1)S(1)}, bf16[256,256]{1,0:T(8,128)(2,1)}, u32[]{:S(2)}) copy-start(bf16[256,256]{1,0:T(8,128)(2,1)} %refs_1_.5) | copy-start | bytes 393220
  0.9 5.6 %copy-start.1 = (s32[3]{0:T(128)S(1)}, s32[3]{0:T(128)}, u32[]{:S(2)}) copy-start(s32[3]{0:T(128)} %param.7) | copy-start | bytes 40
  0.9 4.4 %collective-permute-start.2 = (bf16[256,256]{1,0:T(8,128)(2,1)S(1)}, bf16[256,256]{1,0:T(8,128)(2,1)S(1)}, u32[]{:S(2)}, u32[]{:S(2)}) collective-permute-start(bf16[256,256]{1,0:T(8,128)(2,1)S(1)} %constant_dynamic-update-slice_fusion.refs_3_), channel_id=1, source_target_pairs={{0,4},{2,6},{4,8},{6,10},{8,0},{10,2},{12,16},{14,18},{16,24},{18,... | collective-permute-start | bytes 393224 | tf_op jit(solution)/shard_map/ppermute | solution.py:242
  2.0 4.6 %collective-permute-start = (bf16[256,256]{1,0:T(8,128)(2,1)S(1)}, bf16[256,256]{1,0:T(8,128)(2,1)S(1)}, u32[]{:S(2)}, u32[]{:S(2)}) collective-permute-start(bf16[256,256]{1,0:T(8,128)(2,1)S(1)} %copy-done), channel_id=1, source_target_pairs={{0,2},{2,0},{4,6},{6,4},{8,10},{10,8},{12,14},{14,12},{16,18},{18,... | collective-permute-start | bytes 393224 | tf_op jit(solution)/shard_map/ppermute | solution.py:237
  2.9 7.9 %collective-permute-start.4 = (bf16[256,256]{1,0:T(8,128)(2,1)S(1)}, bf16[256,256]{1,0:T(8,128)(2,1)S(1)}, u32[]{:S(2)}, u32[]{:S(2)}) collective-permute-start(bf16[256,256]{1,0:T(8,128)(2,1)S(1)} %constant_dynamic-update-slice_fusion.refs_3_), channel_id=1, source_target_pairs={{0,2},{2,0},{4,6},{6,4},{8,10},{10,8},{12,20},{14,22},{16,18},{18,... | collective-permute-start | bytes 393224 | tf_op jit(solution)/shard_map/ppermute | solution.py:242
  3.3 7.5 %collective-permute-start.1 = (bf16[256,256]{1,0:T(8,128)(2,1)S(1)}, bf16[256,256]{1,0:T(8,128)(2,1)S(1)}, u32[]{:S(2)}, u32[]{:S(2)}) collective-permute-start(bf16[256,256]{1,0:T(8,128)(2,1)S(1)} %constant_dynamic-update-slice_fusion.refs_3_), channel_id=1, source_target_pairs={{0,8},{2,10},{4,6},{6,4},{8,0},{10,2},{12,28},{14,30},{16,20},{18,... | collective-permute-start | bytes 393224 | tf_op jit(solution)/shard_map/ppermute | solution.py:242
  5.4 5.5 %collective-permute-start.3 = (bf16[256,256]{1,0:T(8,128)(2,1)S(1)}, bf16[256,256]{1,0:T(8,128)(2,1)S(1)}, u32[]{:S(2)}, u32[]{:S(2)}) collective-permute-start(bf16[256,256]{1,0:T(8,128)(2,1)S(1)} %collective-permute-done.2.refs_4_), channel_id=1, source_target_pairs={{0,2},{2,0},{4,6},{6,4},{8,10},{10,8},{12,14},{14,12},{16,24},{18,... | collective-permute-start | bytes 393224 | tf_op jit(solution)/shard_map/ppermute | solution.py:242
  12.7 3.9 %collective-permute-start.5 = (f32[2,136,256]{2,1,0:T(8,128)S(1)}, f32[2,136,256]{2,1,0:T(8,128)S(1)}, u32[]{:S(2)}, u32[]{:S(2)}) collective-permute-start(f32[2,136,256]{2,1,0:T(8,128)S(1)} %get-tuple-element.16), channel_id=1, source_target_pairs={{0,2},{2,0},{4,6},{6,4},{8,10},{10,8},{12,14},{14,12},{16,18},{18,... | collective-permute-start | bytes 835592 | tf_op jit(solution)/shard_map/ppermute | solution.py:253

commit v3 on v2

v3 whole, which is shorter than its diff:
```python
import functools
import math

import jax
import jax.numpy as jnp
from jax import lax
from jax.experimental import pallas as pl
from jax.experimental.pallas import tpu as pltpu
from jax.sharding import PartitionSpec as P

D_HEAD = 128
Q_HEADS = 2
CORES = 2
STAT_ROWS = 8
SCALE = 144.0 ** (-0.5)
FACTOR = SCALE * math.log2(math.e)
MASKED = -1e30
FLOOR = -1e29
NT = (((1,), (1,)), ((), ()))
TN = (((0,), (0,)), ((), ()))


def chip_groups(chips):
    if chips % 8 == 0:
        edge = 3 * chips // 8
        return ((0, edge), (edge, chips))
    return ((0, chips),)


def rotations(chips):
    groups = chip_groups(chips)
    steps = max(high - low for low, high in groups) - 1
    plan = []
    for step in range(steps, 0, -1):
        targets = [0] * chips
        for low, high in groups:
            size = high - low
            turn = step if step < size else 1 + step % (size - 1)
            for chip in range(low, high):
                targets[chip] = low + (chip - low + turn) % size
        plan.append((None, False, targets))
    return plan


def slots_of(chips):
    if chips == 8:
        return [
            (None, False, [1, 2, 0, 4, 6, 7, 3, 5]),
            (None, False, [2, None, 0, 6, 5, 4, 7, 3]),
            (None, False, [None, None, None, 7, None, None, None, 3]),
            (0, False, [None, None, None, None, 5, 4, 7, 6]),
        ]
    return rotations(chips)


def stages_of(chips, count):
    if chips == 8:
        return [[0], [1], [2, 3]]
    return [list(range(low, min(low + 4, count))) for low in range(0, count, 4)]


def over_cores(targets):
    return [
        (CORES * chip + core, CORES * chip + 1 - core if target is None else CORES * target + core)
        for chip, target in enumerate(targets)
        for core in range(CORES)
    ]


def useful_sources(plan):
    had, origins, tables = set(), [], []
    for operand, _, targets in plan:
        origin = list(range(len(targets)))
        for chip, target in enumerate(targets):
            if target is not None:
                origin[target] = chip if operand is None else origins[operand][chip]
        origins.append(origin)
        tables.append(tuple(chip if (source, chip) in had else source for chip, source in enumerate(origin)))
        had.update((source, chip) for chip, source in enumerate(origin))
    for low, high in chip_groups(len(origins[0])):
        for chip in range(low, high):
            assert all((source, chip) in had for source in range(low, chip))
    return tables


def pick(index, table):
    runs = [(0, table[0])]
    for place in range(1, len(table)):
        if table[place] - place != runs[-1][1] - runs[-1][0]:
            runs.append((place, table[place]))
    value = index + (runs[0][1] - runs[0][0])
    for place, entry in runs[1:]:
        value = jnp.where(index >= place, index + (entry - place), value)
    return value


def attend_kernel(tables, widths, first, sides, edge, *refs):
    refs = list(refs)
    starts_ref = refs.pop(0)
    side_q = {side: refs.pop(0) for side in sides}
    blocks = []
    for width in widths:
        parts = [refs.pop(0) for _ in range(width)]
        blocks.append((parts[0].at[:, :D_HEAD], parts[-1].at[:, (D_HEAD if width == 1 else 0) :]))
    olds = None if first else {side: refs.pop(0) for side in sides}
    news = {side: refs.pop(0) for side in sides}
    rows = side_q[sides[0]].shape[0]
    place = lax.axis_index("ctx")
    chip, core = place // CORES, place % CORES
    last_group = chip >= edge
    chunks = [(which, head) for which in sides for head in range(Q_HEADS)]

    def mask_of(which, key_base):
        query_place = place if which == 0 else place + 1 - 2 * core
        query_pos = query_place * rows + lax.broadcasted_iota(jnp.int32, (1, rows), 1)
        low = jnp.zeros_like(query_pos)
        for number in range(starts_ref.shape[1]):
            start = starts_ref[:, number : number + 1]
            low = jnp.where(start <= query_pos, jnp.maximum(start, low), low)
        key_pos = key_base + lax.broadcasted_iota(jnp.int32, (rows, 1), 0)
        return (key_pos <= query_pos) & (key_pos >= low)

    def update(olds, chunks, parts):
        scores = []
        for which, head in chunks:
            queries = side_q[which][:, head * D_HEAD : (head + 1) * D_HEAD]
            row = []
            for block, masks in parts:
                s = lax.dot_general(block[0][...], queries, NT, preferred_element_type=jnp.float32)
                row.append(s if masks is None else jnp.where(masks[which], s, MASKED))
            scores.append(row)
        tops = []
        for (which, head), row in zip(chunks, scores):
            top = functools.reduce(jnp.maximum, [jnp.max(s, axis=0, keepdims=True) for s in row]) * FACTOR
            old_top = FLOOR if olds is None else olds[which][head, D_HEAD : D_HEAD + 1]
            tops.append((jnp.maximum(top, old_top), old_top))
        totals, expos = [], []
        for row, (top, _) in zip(scores, tops):
            row = [jnp.exp2(s * FACTOR - top) for s in row]
            totals.append(functools.reduce(jnp.add, [jnp.sum(expo, axis=0, keepdims=True) for expo in row]))
            expos.append([expo.astype(jnp.bfloat16) for expo in row])
        for (which, head), row, (top, old_top), total in zip(chunks, expos, tops, totals):
            weighted = functools.reduce(
                jnp.add,
                [
                    lax.dot_general(block[1][...], expo, TN, preferred_element_type=jnp.float32)
                    for expo, (block, _) in zip(row, parts)
                ],
            )
            if olds is not None:
                rescale = jnp.exp2(old_top - top)
                total = total + olds[which][head, D_HEAD + 1 : D_HEAD + 2] * rescale
                weighted = weighted + olds[which][head, :D_HEAD] * rescale
            news[which][head, :D_HEAD] = weighted
            news[which][head, D_HEAD : D_HEAD + 1] = top
            news[which][head, D_HEAD + 1 : D_HEAD + 2] = total

    received = []
    for table, block in zip(tables, blocks[len(blocks) - len(tables) :]):
        source = pick(chip, table)
        useful = (source < chip) & ((source >= edge) | (chip < edge))
        received.append((block, source, useful, any(entry < number for number, entry in enumerate(table[:edge]))))

    def one_by_one():
        for block, source, useful, early in received:

            @pl.when(useful & last_group)
            def _(block=block):
                update(news, chunks, [(block, None)])

            if early:

                @pl.when(useful & jnp.logical_not(last_group))
                def _(block=block, source=source):
                    base = (source * CORES + core) * rows
                    update(news, chunks, [(block, {which: mask_of(which, base) for which in sides})])

    if first:
        masks = {which: mask_of(which, place * rows) for which in sides}
        update(None, [chunk for chunk in chunks if chunk[0] == 0], [(blocks[0], masks)])

        @pl.when(core == 0)
        def _():
            update(None, [chunk for chunk in chunks if chunk[0] == 1], [(blocks[0], masks)])

        @pl.when(core == 1)
        def _():
            news[1][...] = jnp.zeros_like(news[1])
            news[1][:, D_HEAD : D_HEAD + 1] = jnp.full((Q_HEADS, 1, rows), FLOOR, jnp.float32)

        one_by_one()
    else:
        patterns = {tuple(edge <= table[chip] < chip for table in tables) for chip in range(edge, len(tables[0]))}
        joint = jnp.bool_(False)
        for pattern in sorted(patterns):
            if sum(pattern) < 2:
                continue
            here = last_group
            for wanted, (_, _, useful, _) in zip(pattern, received):
                here = here & (useful if wanted else jnp.logical_not(useful))
            joint = joint | here

            @pl.when(here)
            def _(pattern=pattern):
                update(olds, chunks, [(entry[0], None) for wanted, entry in zip(pattern, received) if wanted])

        @pl.when(jnp.logical_not(joint))
        def _():
            for which in sides:
                news[which][...] = olds[which][...]
            one_by_one()


def merge_kernel(own_ref, twin_ref, out_ref):
    for head in range(Q_HEADS):
        own_top, twin_top = own_ref[head, D_HEAD : D_HEAD + 1], twin_ref[head, D_HEAD : D_HEAD + 1]
        top = jnp.maximum(own_top, twin_top)
        own_scale, twin_scale = jnp.exp2(own_top - top), jnp.exp2(twin_top - top)
        total = (
            own_ref[head, D_HEAD + 1 : D_HEAD + 2] * own_scale + twin_ref[head, D_HEAD + 1 : D_HEAD + 2] * twin_scale
        )
        result = own_ref[head, :D_HEAD] * (own_scale / total) + twin_ref[head, :D_HEAD] * (twin_scale / total)
        out_ref[:, head * D_HEAD : (head + 1) * D_HEAD] = result.T.astype(jnp.bfloat16)


def vmem_call(kernel, out_shape, operands, flops):
    vmem = pl.BlockSpec(memory_space=pltpu.VMEM)
    return pl.pallas_call(
        kernel,
        out_shape=out_shape,
        in_specs=[vmem] * len(operands),
        out_specs=jax.tree.map(lambda _: vmem, out_shape),
        compiler_params=pltpu.CompilerParams(vmem_limit_bytes=32 * 1024 * 1024),
        cost_estimate=pl.CostEstimate(flops=flops, bytes_accessed=0, transcendentals=0),
    )(*operands)


def shards(count, queries, keys, values, doc_starts):
    chips = count // CORES
    plan = slots_of(chips)
    edge = chip_groups(chips)[-1][0]
    rows = queries.shape[0]
    swap = [(place, place + 1 - 2 * (place % CORES)) for place in range(count)]
    seen = useful_sources(plan)
    starts = doc_starts.reshape(1, -1)
    own = {True: (keys, values), False: (jnp.concatenate([keys, values], axis=1),)}
    arrived = []
    for operand, split, targets in plan:
        block = own[split] if operand is None else arrived[operand]
        arrived.append(tuple(lax.ppermute(part, "ctx", over_cores(targets)) for part in block))
    both = (queries, lax.ppermute(queries, "ctx", swap))
    partial = jax.ShapeDtypeStruct((Q_HEADS, D_HEAD + STAT_ROWS, rows), jnp.float32)
    stages = stages_of(chips, len(plan))
    state = ()
    for number, slots in enumerate(stages):
        blocks = ([] if state else [own[plan[0][1]]]) + [arrived[slot] for slot in slots]
        widths = [len(block) for block in blocks]
        tables = [seen[slot] for slot in slots]
        new = [None, None]
        for sides in [(1,), (0,)] if number == len(stages) - 1 and state else [(0, 1)]:
            flops = len(blocks) * len(sides) * Q_HEADS * rows * rows * D_HEAD * 4
            kernel = functools.partial(attend_kernel, tables, widths, not state, sides, edge)
            operands = [starts, *(both[side] for side in sides), *(part for block in blocks for part in block)]
            operands += [state[side] for side in sides] if state else []
            for side, result in zip(sides, vmem_call(kernel, (partial,) * len(sides), operands, flops)):
                new[side] = result
        state = tuple(new)
    mine, others = state
    out_shape = jax.ShapeDtypeStruct(queries.shape, jnp.bfloat16)
    return vmem_call(merge_kernel, out_shape, (mine, lax.ppermute(others, "ctx", swap)), 1000)


def solution(mesh):
    return jax.shard_map(
        functools.partial(shards, mesh.shape["ctx"]),
        mesh=mesh,
        in_specs=(P("ctx", "head"), P("ctx", "head"), P("ctx", "head"), P("head")),
        out_specs=P("ctx", "head"),
        check_vma=False,
    )
```

time: 17.4 us -> 16.2 us (0.931)
  starting transfers between devices: 6.35 us -> 4.46 us
  waiting for transfers between devices: 5.22 us -> 6.77 us
  Pallas kernels: 4.72 us -> 3.8 us
    ppermute x5, waiting for transfers between devices: 4.04 us -> 6.13 us  [the longest x4 6.13 us: shards(): lax.ppermute(part, 'ctx', over_cores(targets))]
    ppermute x1, starting transfers between devices: 2.67 us -> 0.58 us  [shards(): lax.ppermute(others, 'ctx', swap)]
    pallas_call x4 -> x5, Pallas kernels: 4.72 us -> 3.8 us  [vmem_call(): pl.pallas_call(kernel, out_shape=out_shape, in_specs=[vmem] * len(operand...]
    ppermute x1, waiting for transfers between devices: 1.19 us -> 0.64 us  [shards(): lax.ppermute(others, 'ctx', swap)]
    ppermute x5, starting transfers between devices: 3.69 us -> 3.88 us  [the longest x4 2.93 us: shards(): lax.ppermute(part, 'ctx', over_cores(targets))]
  transfers between devices with their start and end apart: 6 -> 6, of which waited for: 3 -> 4; matrix products, arithmetic and copies ran while one was open for 0% -> 0% of each run, Pallas kernels for 12% -> 16%
where the time goes in v3:
time: 16.2 us; the launch traced here: 16 us
  waiting for transfers between devices  6.77 us (42%)
  starting transfers between devices  4.46 us (28%)
  Pallas kernels  3.8 us (23%)
  local copies, waits for them, and re-layouts  0.92 us (6%)
    ppermute x4, waiting for transfers between devices, shards(): lax.ppermute(part, 'ctx', over_cores(targets))  6.13 us
    pallas_call x5, Pallas kernels, vmem_call(): pl.pallas_call(kernel, out_shape=out_shape, in_specs=[vmem] * len(operand...  3.8 us
    ppermute x4, starting transfers between devices, shards(): lax.ppermute(part, 'ctx', over_cores(targets))  2.93 us
    ppermute x1, starting transfers between devices, shards(): both = (queries, lax.ppermute(queries, 'ctx', swap))  0.96 us
    unnamed x7, local copies, waits for them, and re-layouts  0.9 us
    ppermute x1, waiting for transfers between devices, shards(): lax.ppermute(others, 'ctx', swap)  0.64 us
    ppermute x1, starting transfers between devices, shards(): lax.ppermute(others, 'ctx', swap)  0.58 us
  transfers between devices with their start and end apart: 6, of which 4 were waited for; matrix products, arithmetic and copies ran while one was open for 0% of the time, Pallas kernels for 16%

profile of v3, /device:TPU:25, one launch (start us, length us, event | category | flops | bytes accessed | tf_op | source)
XLA Modules:
  0.0 16.0 jit_solution(13127982306673876958)
XLA Ops:
  0.0 0.0 copy-start.2
  0.0 0.0 copy-start
  0.0 0.9 %constant_dynamic-update-slice_fusion.1 = bf16[256,256]{1,0:T(8,128)(2,1)S(1)} fusion(bf16[256,128]{1,0:T(8,128)(2,1)} %param.5), kind=kLoop, calls=%fused_computation.1 | loop fusion | bytes 131072
  0.9 0.0 copy-done.2
  0.9 0.0 copy-start.1
  0.9 1.0 %collective-permute-start.1 = (bf16[256,256]{1,0:T(8,128)(2,1)S(1)}, bf16[256,256]{1,0:T(8,128)(2,1)S(1)}, u32[]{:S(2)}, u32[]{:S(2)}) collective-permute-start(bf16[256,256]{1,0:T(8,128)(2,1)S(1)} %constant_dynamic-update-slice_fusion.refs_3_), channel_id=1, source_target_pairs={{0,4},{2,6},{4,8},{6,10},{8,0},{10,2},{12,16},{14,18},{16,24},{18,... | collective-permute-start | bytes 393224 | tf_op jit(solution)/shard_map/ppermute | solution.py:250
  2.0 0.0 copy-done
  2.0 1.0 %collective-permute-start.3 = (bf16[256,256]{1,0:T(8,128)(2,1)S(1)}, bf16[256,256]{1,0:T(8,128)(2,1)S(1)}, u32[]{:S(2)}, u32[]{:S(2)}) collective-permute-start(bf16[256,256]{1,0:T(8,128)(2,1)S(1)} %copy-done), channel_id=1, source_target_pairs={{0,2},{2,0},{4,6},{6,4},{8,10},{10,8},{12,14},{14,12},{16,18},{18,... | collective-permute-start | bytes 393224 | tf_op jit(solution)/shard_map/ppermute | solution.py:251
  2.9 0.4 %collective-permute-start.4 = (bf16[256,256]{1,0:T(8,128)(2,1)S(1)}, bf16[256,256]{1,0:T(8,128)(2,1)S(1)}, u32[]{:S(2)}, u32[]{:S(2)}) collective-permute-start(bf16[256,256]{1,0:T(8,128)(2,1)S(1)} %constant_dynamic-update-slice_fusion.refs_3_), channel_id=1, source_target_pairs={{0,8},{2,10},{4,6},{6,4},{8,0},{10,2},{12,24},{14,26},{16,20},{18,... | collective-permute-start | bytes 393224 | tf_op jit(solution)/shard_map/ppermute | solution.py:250
  3.3 0.3 %collective-permute-start = (bf16[256,256]{1,0:T(8,128)(2,1)S(1)}, bf16[256,256]{1,0:T(8,128)(2,1)S(1)}, u32[]{:S(2)}, u32[]{:S(2)}) collective-permute-start(bf16[256,256]{1,0:T(8,128)(2,1)S(1)} %constant_dynamic-update-slice_fusion.refs_3_), channel_id=1, source_target_pairs={{0,2},{2,0},{4,6},{6,4},{8,10},{10,8},{12,28},{14,30},{16,18},{18,... | collective-permute-start | bytes 393224 | tf_op jit(solution)/shard_map/ppermute | solution.py:250
  3.6 1.7 %collective-permute-done.1.refs_4_ = bf16[256,256]{1,0:T(8,128)(2,1)S(1)} collective-permute-done((bf16[256,256]{1,0:T(8,128)(2,1)S(1)}, bf16[256,256]{1,0:T(8,128)(2,1)S(1)}, u32[]{:S(2)}, u32[]{:S(2)}) %collective-permute-start.1) | collective-permute-done | bytes 131104 | tf_op jit(solution)/shard_map/ppermute | solution.py:250
  5.4 1.2 %collective-permute-start.2 = (bf16[256,256]{1,0:T(8,128)(2,1)S(1)}, bf16[256,256]{1,0:T(8,128)(2,1)S(1)}, u32[]{:S(2)}, u32[]{:S(2)}) collective-permute-start(bf16[256,256]{1,0:T(8,128)(2,1)S(1)} %collective-permute-done.1.refs_4_), channel_id=1, source_target_pairs={{0,2},{2,0},{4,6},{6,4},{8,10},{10,8},{12,14},{14,12},{16,20},{18,... | collective-permute-start | bytes 393224 | tf_op jit(solution)/shard_map/ppermute | solution.py:250
  6.6 0.0 collective-permute-done.3.refs_2_.refs_1_
  6.6 0.0 copy-done.1
  6.6 1.2 %shard_map.46 = (f32[2,136,256]{2,1,0:T(8,128)S(1)}, f32[2,136,256]{2,1,0:T(8,128)S(1)}) custom-call(s32[1,3]{1,0:T(1,128)S(1)} %bitcast.1, bf16[256,256]{1,0:T(8,128)(2,1)S(1)} %copy-done, bf16[256,256]{1,0:T(8,128)(2,1)S(1)} %collective-permute-done.3.refs_2_.refs_1_, bf16[256,256]{1,0:T(8,128)(2,1)S(1)} %constant_dynamic-update-slice_fusion.refs_3_, ...), custom_call_target="tpu_custom_call" | custom-call | flops 268435456 | tf_op jit(solution)/shard_map/pallas_call | solution.py:228
  7.8 2.1 %collective-permute-done.4.refs_3_ = bf16[256,256]{1,0:T(8,128)(2,1)S(1)} collective-permute-done((bf16[256,256]{1,0:T(8,128)(2,1)S(1)}, bf16[256,256]{1,0:T(8,128)(2,1)S(1)}, u32[]{:S(2)}, u32[]{:S(2)}) %collective-permute-start.4) | collective-permute-done | bytes 131104 | tf_op jit(solution)/shard_map/ppermute | solution.py:250
  9.9 0.7 %shard_map.47 = (f32[2,136,256]{2,1,0:T(8,128)S(1)}, f32[2,136,256]{2,1,0:T(8,128)S(1)}) custom-call(s32[1,3]{1,0:T(1,128)S(1)} %bitcast.2, bf16[256,256]{1,0:T(8,128)(2,1)S(1)} %copy-done, bf16[256,256]{1,0:T(8,128)(2,1)S(1)} %collective-permute-done.3.refs_2_.refs_1_, bf16[256,256]{1,0:T(8,128)(2,1)S(1)} %collective-permute-done.4.refs_3_, ...), custom_call_target="tpu_custom_call" | custom-call | flops 134217728 | tf_op jit(solution)/shard_map/pallas_call | solution.py:228
  10.6 0.0 collective-permute-done.refs_2_
  10.6 2.3 %collective-permute-done.2.refs_3_ = bf16[256,256]{1,0:T(8,128)(2,1)S(1)} collective-permute-done((bf16[256,256]{1,0:T(8,128)(2,1)S(1)}, bf16[256,256]{1,0:T(8,128)(2,1)S(1)}, u32[]{:S(2)}, u32[]{:S(2)}) %collective-permute-start.2) | collective-permute-done | bytes 131104 | tf_op jit(solution)/shard_map/ppermute | solution.py:250
  12.9 0.5 %shard_map.49 = f32[2,136,256]{2,1,0:T(8,128)S(1)} custom-call(s32[1,3]{1,0:T(1,128)S(1)} %bitcast.3, bf16[256,256]{1,0:T(8,128)(2,1)S(1)} %collective-permute-done.3.refs_2_.refs_1_, bf16[256,256]{1,0:T(8,128)(2,1)S(1)} %collective-permute-done.refs_2_, bf16[256,256]{1,0:T(8,128)(2,1)S(1)} %collective-permute-done.2.refs_3_, ...), custom_call_target="tpu_custom_call" | custom-call | flops 134217728 | tf_op jit(solution)/shard_map/pallas_call | solution.py:228
  13.5 0.6 %collective-permute-start.5 = (f32[2,136,256]{2,1,0:T(8,128)S(1)}, f32[2,136,256]{2,1,0:T(8,128)S(1)}, u32[]{:S(2)}, u32[]{:S(2)}) collective-permute-start(f32[2,136,256]{2,1,0:T(8,128)S(1)} %shard_map.49), channel_id=1, source_target_pairs={{0,2},{2,0},{4,6},{6,4},{8,10},{10,8},{12,14},{14,12},{16,18},{18,... | collective-permute-start | bytes 835592 | tf_op jit(solution)/shard_map/ppermute | solution.py:270
  14.1 0.5 %shard_map.48.own_ref = f32[2,136,256]{2,1,0:T(8,128)S(1)} custom-call(s32[1,3]{1,0:T(1,128)S(1)} %bitcast.4, bf16[256,256]{1,0:T(8,128)(2,1)S(1)} %copy-done, bf16[256,256]{1,0:T(8,128)(2,1)S(1)} %collective-permute-done.refs_2_, bf16[256,256]{1,0:T(8,128)(2,1)S(1)} %collective-permute-done.2.refs_3_, f32[2,136,256]{2,1,0:T(8,128)S(1)} %get-tuple-element.11.refs_4_), custom_call_target="tpu_custom_call" | custom-call | flops 134217728 | tf_op jit(solution)/shard_map/pallas_call | solution.py:228
  14.6 0.6 %collective-permute-done.5.twin_ref = f32[2,136,256]{2,1,0:T(8,128)S(1)} collective-permute-done((f32[2,136,256]{2,1,0:T(8,128)S(1)}, f32[2,136,256]{2,1,0:T(8,128)S(1)}, u32[]{:S(2)}, u32[]{:S(2)}) %collective-permute-start.5) | collective-permute-done | bytes 278560 | tf_op jit(solution)/shard_map/ppermute | solution.py:270
  15.2 0.8 %shard_map.50 = bf16[256,256]{1,0:T(8,128)(2,1)} custom-call(f32[2,136,256]{2,1,0:T(8,128)S(1)} %shard_map.48.own_ref, f32[2,136,256]{2,1,0:T(8,128)S(1)} %collective-permute-done.5.twin_ref), custom_call_target="tpu_custom_call" | custom-call | flops 1000 | tf_op jit(solution)/shard_map/pallas_call | solution.py:228
  (1 shorter events, 0.0 us)
Async XLA Ops:
  0.0 0.9 %copy-start.2 = (bf16[256,128]{1,0:T(8,128)(2,1)S(1)}, bf16[256,128]{1,0:T(8,128)(2,1)}, u32[]{:S(2)}) copy-start(bf16[256,128]{1,0:T(8,128)(2,1)} %param.6) | copy-start | bytes 196612
  0.0 2.0 %copy-start = (bf16[256,256]{1,0:T(8,128)(2,1)S(1)}, bf16[256,256]{1,0:T(8,128)(2,1)}, u32[]{:S(2)}) copy-start(bf16[256,256]{1,0:T(8,128)(2,1)} %refs_1_.5) | copy-start | bytes 393220
  0.9 5.6 %copy-start.1 = (s32[3]{0:T(128)S(1)}, s32[3]{0:T(128)}, u32[]{:S(2)}) copy-start(s32[3]{0:T(128)} %param.7) | copy-start | bytes 40
  0.9 4.4 %collective-permute-start.1 = (bf16[256,256]{1,0:T(8,128)(2,1)S(1)}, bf16[256,256]{1,0:T(8,128)(2,1)S(1)}, u32[]{:S(2)}, u32[]{:S(2)}) collective-permute-start(bf16[256,256]{1,0:T(8,128)(2,1)S(1)} %constant_dynamic-update-slice_fusion.refs_3_), channel_id=1, source_target_pairs={{0,4},{2,6},{4,8},{6,10},{8,0},{10,2},{12,16},{14,18},{16,24},{18,... | collective-permute-start | bytes 393224 | tf_op jit(solution)/shard_map/ppermute | solution.py:250
  2.0 4.6 %collective-permute-start.3 = (bf16[256,256]{1,0:T(8,128)(2,1)S(1)}, bf16[256,256]{1,0:T(8,128)(2,1)S(1)}, u32[]{:S(2)}, u32[]{:S(2)}) collective-permute-start(bf16[256,256]{1,0:T(8,128)(2,1)S(1)} %copy-done), channel_id=1, source_target_pairs={{0,2},{2,0},{4,6},{6,4},{8,10},{10,8},{12,14},{14,12},{16,18},{18,... | collective-permute-start | bytes 393224 | tf_op jit(solution)/shard_map/ppermute | solution.py:251
  2.9 6.9 %collective-permute-start.4 = (bf16[256,256]{1,0:T(8,128)(2,1)S(1)}, bf16[256,256]{1,0:T(8,128)(2,1)S(1)}, u32[]{:S(2)}, u32[]{:S(2)}) collective-permute-start(bf16[256,256]{1,0:T(8,128)(2,1)S(1)} %constant_dynamic-update-slice_fusion.refs_3_), channel_id=1, source_target_pairs={{0,8},{2,10},{4,6},{6,4},{8,0},{10,2},{12,24},{14,26},{16,20},{18,... | collective-permute-start | bytes 393224 | tf_op jit(solution)/shard_map/ppermute | solution.py:250
  3.3 7.3 %collective-permute-start = (bf16[256,256]{1,0:T(8,128)(2,1)S(1)}, bf16[256,256]{1,0:T(8,128)(2,1)S(1)}, u32[]{:S(2)}, u32[]{:S(2)}) collective-permute-start(bf16[256,256]{1,0:T(8,128)(2,1)S(1)} %constant_dynamic-update-slice_fusion.refs_3_), channel_id=1, source_target_pairs={{0,2},{2,0},{4,6},{6,4},{8,10},{10,8},{12,28},{14,30},{16,18},{18,... | collective-permute-start | bytes 393224 | tf_op jit(solution)/shard_map/ppermute | solution.py:250
  5.4 7.6 %collective-permute-start.2 = (bf16[256,256]{1,0:T(8,128)(2,1)S(1)}, bf16[256,256]{1,0:T(8,128)(2,1)S(1)}, u32[]{:S(2)}, u32[]{:S(2)}) collective-permute-start(bf16[256,256]{1,0:T(8,128)(2,1)S(1)} %collective-permute-done.1.refs_4_), channel_id=1, source_target_pairs={{0,2},{2,0},{4,6},{6,4},{8,10},{10,8},{12,14},{14,12},{16,20},{18,... | collective-permute-start | bytes 393224 | tf_op jit(solution)/shard_map/ppermute | solution.py:250
  13.5 1.8 %collective-permute-start.5 = (f32[2,136,256]{2,1,0:T(8,128)S(1)}, f32[2,136,256]{2,1,0:T(8,128)S(1)}, u32[]{:S(2)}, u32[]{:S(2)}) collective-permute-start(f32[2,136,256]{2,1,0:T(8,128)S(1)} %shard_map.49), channel_id=1, source_target_pairs={{0,2},{2,0},{4,6},{6,4},{8,10},{10,8},{12,14},{14,12},{16,18},{18,... | collective-permute-start | bytes 835592 | tf_op jit(solution)/shard_map/ppermute | solution.py:270

commit v4 on v3

--- a/solution.py
+++ b/solution.py
@@ -12,6 +12,8 @@
 Q_HEADS = 2
 CORES = 2
 STAT_ROWS = 8
+PACKED_ROWS = 16
+PIECES = 3
 SCALE = 144.0 ** (-0.5)
 FACTOR = SCALE * math.log2(math.e)
 MASKED = -1e30
@@ -38,24 +40,25 @@
             turn = step if step < size else 1 + step % (size - 1)
             for chip in range(low, high):
                 targets[chip] = low + (chip - low + turn) % size
-        plan.append((None, False, targets))
+        plan.append((None, False, targets, None))
     return plan
 
 
 def slots_of(chips):
     if chips == 8:
         return [
-            (None, False, [1, 2, 0, 4, 6, 7, 3, 5]),
-            (None, False, [2, None, 0, 6, 5, 4, 7, 3]),
-            (None, False, [None, None, None, 7, None, None, None, 3]),
-            (0, False, [None, None, None, None, 5, 4, 7, 6]),
+            (None, True, [1, 2, 0, 4, 6, 7, 3, 5], None),
+            (None, False, [2, None, 0, 7, 5, 4, None, 3], None),
+            (None, False, [None, None, None, 5, None, 3, 7, 6], None),
+            (0, False, [None, None, None, None, None, None, 7, 6], None),
+            (0, False, [None, None, None, None, 6, None, 4, None], None),
         ]
     return rotations(chips)
 
 
 def stages_of(chips, count):
     if chips == 8:
-        return [[0], [1], [2, 3]]
+        return [[0], [1], [2], [4], [3]]
     return [list(range(low, min(low + 4, count))) for low in range(0, count, 4)]
 
 
@@ -69,7 +72,7 @@
 
 def useful_sources(plan):
     had, origins, tables = set(), [], []
-    for operand, _, targets in plan:
+    for operand, _, targets, _ in plan:
         origin = list(range(len(targets)))
         for chip, target in enumerate(targets):
             if target is not None:
@@ -94,8 +97,18 @@
     return value
 
 
-def attend_kernel(tables, widths, first, sides, edge, *refs):
+def pieces_of(row):
+    pieces = []
+    for _ in range(PIECES):
+        pieces.append(row.astype(jnp.bfloat16))
+        row = row - pieces[-1].astype(jnp.float32)
+    return pieces
+
+
+def attend_kernel(tables, widths, first, sides, edge, packed, *refs):
     refs = list(refs)
+    if packed:
+        work = refs.pop()
     starts_ref = refs.pop(0)
     side_q = {side: refs.pop(0) for side in sides}
     blocks = []
@@ -103,7 +116,8 @@
         parts = [refs.pop(0) for _ in range(width)]
         blocks.append((parts[0].at[:, :D_HEAD], parts[-1].at[:, (D_HEAD if width == 1 else 0) :]))
     olds = None if first else {side: refs.pop(0) for side in sides}
-    news = {side: refs.pop(0) for side in sides}
+    outs = {side: refs.pop(0) for side in sides}
+    news = {sides[0]: work} if packed else outs
     rows = side_q[sides[0]].shape[0]
     place = lax.axis_index("ctx")
     chip, core = place // CORES, place % CORES
@@ -210,26 +224,39 @@
                 news[which][...] = olds[which][...]
             one_by_one()
 
+    if packed:
+        for head in range(Q_HEADS):
+            low = []
+            for row in (D_HEAD, D_HEAD + 1):
+                low += pieces_of(work[head, row : row + 1])
+            low.append(jnp.zeros((PACKED_ROWS - 2 * PIECES, rows), jnp.bfloat16))
+            outs[sides[0]][head, :D_HEAD] = work[head, :D_HEAD].astype(jnp.bfloat16)
+            outs[sides[0]][head, D_HEAD:] = jnp.concatenate(low, axis=0)
+
 
 def merge_kernel(own_ref, twin_ref, out_ref):
     for head in range(Q_HEADS):
-        own_top, twin_top = own_ref[head, D_HEAD : D_HEAD + 1], twin_ref[head, D_HEAD : D_HEAD + 1]
+        low = twin_ref[head, D_HEAD:].astype(jnp.float32)
+        rows_of = [low[number : number + 1] for number in range(2 * PIECES)]
+        twin_top = functools.reduce(jnp.add, rows_of[:PIECES])
+        twin_total = functools.reduce(jnp.add, rows_of[PIECES:])
+        own_top = own_ref[head, D_HEAD : D_HEAD + 1]
         top = jnp.maximum(own_top, twin_top)
         own_scale, twin_scale = jnp.exp2(own_top - top), jnp.exp2(twin_top - top)
-        total = (
-            own_ref[head, D_HEAD + 1 : D_HEAD + 2] * own_scale + twin_ref[head, D_HEAD + 1 : D_HEAD + 2] * twin_scale
-        )
-        result = own_ref[head, :D_HEAD] * (own_scale / total) + twin_ref[head, :D_HEAD] * (twin_scale / total)
+        total = own_ref[head, D_HEAD + 1 : D_HEAD + 2] * own_scale + twin_total * twin_scale
+        twin = twin_ref[head, :D_HEAD].astype(jnp.float32)
+        result = own_ref[head, :D_HEAD] * (own_scale / total) + twin * (twin_scale / total)
         out_ref[:, head * D_HEAD : (head + 1) * D_HEAD] = result.T.astype(jnp.bfloat16)
 
 
-def vmem_call(kernel, out_shape, operands, flops):
+def vmem_call(kernel, out_shape, operands, flops, scratch=()):
     vmem = pl.BlockSpec(memory_space=pltpu.VMEM)
     return pl.pallas_call(
         kernel,
         out_shape=out_shape,
         in_specs=[vmem] * len(operands),
         out_specs=jax.tree.map(lambda _: vmem, out_shape),
+        scratch_shapes=scratch,
         compiler_params=pltpu.CompilerParams(vmem_limit_bytes=32 * 1024 * 1024),
         cost_estimate=pl.CostEstimate(flops=flops, bytes_accessed=0, transcendentals=0),
     )(*operands)
@@ -245,11 +272,16 @@
     starts = doc_starts.reshape(1, -1)
     own = {True: (keys, values), False: (jnp.concatenate([keys, values], axis=1),)}
     arrived = []
-    for operand, split, targets in plan:
+    for operand, split, targets, after in plan:
         block = own[split] if operand is None else arrived[operand]
+        if len(block) > 1 and not split:
+            block = (jnp.concatenate(block, axis=1),)
+        if after is not None:
+            block = lax.optimization_barrier((*block, *arrived[after]))[: len(block)]
         arrived.append(tuple(lax.ppermute(part, "ctx", over_cores(targets)) for part in block))
     both = (queries, lax.ppermute(queries, "ctx", swap))
     partial = jax.ShapeDtypeStruct((Q_HEADS, D_HEAD + STAT_ROWS, rows), jnp.float32)
+    to_send = jax.ShapeDtypeStruct((Q_HEADS, D_HEAD + PACKED_ROWS, rows), jnp.bfloat16)
     stages = stages_of(chips, len(plan))
     state = ()
     for number, slots in enumerate(stages):
@@ -257,12 +289,16 @@
         widths = [len(block) for block in blocks]
         tables = [seen[slot] for slot in slots]
         new = [None, None]
-        for sides in [(1,), (0,)] if number == len(stages) - 1 and state else [(0, 1)]:
+        last = number == len(stages) - 1
+        for sides in [(1,), (0,)] if last and state else [(0, 1)]:
             flops = len(blocks) * len(sides) * Q_HEADS * rows * rows * D_HEAD * 4
-            kernel = functools.partial(attend_kernel, tables, widths, not state, sides, edge)
+            packed = last and sides == (1,)
+            kernel = functools.partial(attend_kernel, tables, widths, not state, sides, edge, packed)
             operands = [starts, *(both[side] for side in sides), *(part for block in blocks for part in block)]
             operands += [state[side] for side in sides] if state else []
-            for side, result in zip(sides, vmem_call(kernel, (partial,) * len(sides), operands, flops)):
+            out_shape = (to_send if packed else partial,) * len(sides)
+            scratch = [pltpu.VMEM(partial.shape, partial.dtype)] if packed else []
+            for side, result in zip(sides, vmem_call(kernel, out_shape, operands, flops, scratch)):
                 new[side] = result
         state = tuple(new)
     mine, others = state

time: 16.2 us -> 16 us (0.988)
  waiting for transfers between devices: 6.77 us -> 3.54 us
  starting transfers between devices: 4.46 us -> 7.34 us
    ppermute x4 -> x6, waiting for transfers between devices: 6.13 us -> 2.95 us  [shards(): lax.ppermute(part, 'ctx', over_cores(targets))]
    ppermute x4 -> x6, starting transfers between devices: 2.93 us -> 4.67 us  [shards(): lax.ppermute(part, 'ctx', over_cores(targets))]
    ppermute x1, starting transfers between devices: 0.96 us -> 1.8 us  [shards(): both = (queries, lax.ppermute(queries, 'ctx', swap))]
    ppermute x1, starting transfers between devices: 0.58 us -> 0.87 us  [shards(): lax.ppermute(others, 'ctx', swap)]
    ppermute x1, waiting for transfers between devices: 0.64 us -> 0.47 us  [shards(): lax.ppermute(others, 'ctx', swap)]
    pallas_call x5 -> x7, Pallas kernels: 3.8 us -> 3.93 us  [vmem_call(): pl.pallas_call(kernel, out_shape=out_shape, in_specs=[vmem] * len(operand...]
    unnamed x7 -> x10, local copies, waits for them, and re-layouts: 0.9 us -> 0.88 us
  transfers between devices with their start and end apart: 6 -> 8, of which waited for: 4 -> 4; matrix products, arithmetic and copies ran while one was open for 0% -> 6% of each run, Pallas kernels for 16% -> 16%
where the time goes in v4:
time: 16 us; the launch traced here: 15.9 us
  starting transfers between devices  7.34 us (46%)
  Pallas kernels  3.93 us (25%)
  waiting for transfers between devices  3.54 us (22%)
  local copies, waits for them, and re-layouts  0.92 us (6%)
    ppermute x6, starting transfers between devices, shards(): lax.ppermute(part, 'ctx', over_cores(targets))  4.67 us
    pallas_call x7, Pallas kernels, vmem_call(): pl.pallas_call(kernel, out_shape=out_shape, in_specs=[vmem] * len(operand...  3.93 us
    ppermute x6, waiting for transfers between devices, shards(): lax.ppermute(part, 'ctx', over_cores(targets))  2.95 us
    ppermute x1, starting transfers between devices, shards(): both = (queries, lax.ppermute(queries, 'ctx', swap))  1.8 us
    unnamed x10, local copies, waits for them, and re-layouts  0.88 us
    ppermute x1, starting transfers between devices, shards(): lax.ppermute(others, 'ctx', swap)  0.87 us
    ppermute x1, waiting for transfers between devices, shards(): lax.ppermute(others, 'ctx', swap)  0.47 us
  transfers between devices with their start and end apart: 8, of which 4 were waited for; matrix products, arithmetic and copies ran while one was open for 6% of the time, Pallas kernels for 16%

profile of v4, /device:TPU:25, one launch (start us, length us, event | category | flops | bytes accessed | tf_op | source)
XLA Modules:
  0.0 15.9 jit_solution(3623812083597640058)
XLA Ops:
  0.0 0.0 copy-start.2
  0.0 0.0 copy-start
  0.0 1.0 %collective-permute-start = (bf16[256,128]{1,0:T(8,128)(2,1)}, bf16[256,128]{1,0:T(8,128)(2,1)S(1)}, u32[]{:S(2)}, u32[]{:S(2)}) collective-permute-start(bf16[256,128]{1,0:T(8,128)(2,1)} %refs_3_.1), channel_id=1, source_target_pairs={{0,4},{2,6},{4,8},{6,10},{8,0},{10,2},{12,16},{14,18},{16,24},{18,... | collective-permute-start | bytes 196616 | tf_op jit(solution)/shard_map/ppermute | solution.py:281
  1.0 1.3 %collective-permute-start.1 = (bf16[256,128]{1,0:T(8,128)(2,1)}, bf16[256,128]{1,0:T(8,128)(2,1)S(1)}, u32[]{:S(2)}, u32[]{:S(2)}) collective-permute-start(bf16[256,128]{1,0:T(8,128)(2,1)} %refs_4_.1), channel_id=1, source_target_pairs={{0,4},{2,6},{4,8},{6,10},{8,0},{10,2},{12,16},{14,18},{16,24},{18,... | collective-permute-start | bytes 196616 | tf_op jit(solution)/shard_map/ppermute | solution.py:281
  2.3 0.9 %constant_dynamic-update-slice_fusion.3 = bf16[256,256]{1,0:T(8,128)(2,1)S(1)} fusion(bf16[256,128]{1,0:T(8,128)(2,1)} %refs_3_.1), kind=kLoop, calls=%fused_computation.3 | loop fusion | bytes 131072
  3.1 0.0 copy-done.2
  3.1 1.3 %collective-permute-start.6 = (bf16[256,256]{1,0:T(8,128)(2,1)S(1)}, bf16[256,256]{1,0:T(8,128)(2,1)S(1)}, u32[]{:S(2)}, u32[]{:S(2)}) collective-permute-start(bf16[256,256]{1,0:T(8,128)(2,1)S(1)} %constant_dynamic-update-slice_fusion.2), channel_id=1, source_target_pairs={{0,8},{2,10},{4,6},{6,4},{8,0},{10,2},{12,28},{14,30},{16,20},{18,... | collective-permute-start | bytes 393224 | tf_op jit(solution)/shard_map/ppermute | solution.py:281
  4.4 0.3 %collective-permute-start.5 = (bf16[256,256]{1,0:T(8,128)(2,1)S(1)}, bf16[256,256]{1,0:T(8,128)(2,1)S(1)}, u32[]{:S(2)}, u32[]{:S(2)}) collective-permute-start(bf16[256,256]{1,0:T(8,128)(2,1)S(1)} %constant_dynamic-update-slice_fusion.2), channel_id=1, source_target_pairs={{0,2},{2,0},{4,6},{6,4},{8,10},{10,8},{12,20},{14,22},{16,18},{18,... | collective-permute-start | bytes 393224 | tf_op jit(solution)/shard_map/ppermute | solution.py:281
  4.8 0.0 copy-done
  4.8 1.8 %collective-permute-start.3 = (bf16[256,256]{1,0:T(8,128)(2,1)S(1)}, bf16[256,256]{1,0:T(8,128)(2,1)S(1)}, u32[]{:S(2)}, u32[]{:S(2)}) collective-permute-start(bf16[256,256]{1,0:T(8,128)(2,1)S(1)} %copy-done), channel_id=1, source_target_pairs={{0,2},{2,0},{4,6},{6,4},{8,10},{10,8},{12,14},{14,12},{16,18},{18,... | collective-permute-start | bytes 393224 | tf_op jit(solution)/shard_map/ppermute | solution.py:282
  6.6 0.0 collective-permute-done.refs_5_
  6.6 0.0 copy-start.1
  6.6 0.0 collective-permute-done.1.refs_6_
  6.7 0.0 copy-start.3
  6.7 0.1 collective-permute-start.4
  6.7 0.7 %collective-permute-start.2 = (bf16[256,256]{1,0:T(8,128)(2,1)S(1)}, bf16[256,256]{1,0:T(8,128)(2,1)S(1)}, u32[]{:S(2)}, u32[]{:S(2)}) collective-permute-start(bf16[256,256]{1,0:T(8,128)(2,1)S(1)} %constant_dynamic-update-slice_fusion), channel_id=1, source_target_pairs={{0,2},{2,0},{4,6},{6,4},{8,10},{10,8},{12,14},{14,12},{16,18},{18,... | collective-permute-start | bytes 393224 | tf_op jit(solution)/shard_map/ppermute | solution.py:281
  7.5 0.1 collective-permute-done.3.refs_2_.refs_1_
  7.6 0.0 copy-done.1
  7.6 0.0 copy-done.3
  7.6 1.2 %shard_map.46 = (f32[2,136,256]{2,1,0:T(8,128)S(1)}, f32[2,136,256]{2,1,0:T(8,128)S(1)}) custom-call(s32[1,3]{1,0:T(1,128)S(1)} %bitcast.1, bf16[256,256]{1,0:T(8,128)(2,1)S(1)} %copy-done, bf16[256,256]{1,0:T(8,128)(2,1)S(1)} %collective-permute-done.3.refs_2_.refs_1_, bf16[256,128]{1,0:T(8,128)(2,1)S(1)} %copy-done.1, bf16[256,128]{1,0:T(8,128)(2,1)S(1)} %copy-done.2, ...), custom_call_target="tpu_custom_call" | custom-call | flops 268435456 | tf_op jit(solution)/shard_map/pallas_call | solution.py:254
  8.8 0.0 collective-permute-done.6.refs_3_
  8.9 0.6 %collective-permute-done.5.refs_3_ = bf16[256,256]{1,0:T(8,128)(2,1)S(1)} collective-permute-done((bf16[256,256]{1,0:T(8,128)(2,1)S(1)}, bf16[256,256]{1,0:T(8,128)(2,1)S(1)}, u32[]{:S(2)}, u32[]{:S(2)}) %collective-permute-start.5) | collective-permute-done | bytes 131104 | tf_op jit(solution)/shard_map/ppermute | solution.py:281
  9.5 2.3 %collective-permute-done.4.refs_3_ = bf16[256,256]{1,0:T(8,128)(2,1)S(1)} collective-permute-done((bf16[256,256]{1,0:T(8,128)(2,1)S(1)}, bf16[256,256]{1,0:T(8,128)(2,1)S(1)}, u32[]{:S(2)}, u32[]{:S(2)}) %collective-permute-start.4) | collective-permute-done | bytes 131104 | tf_op jit(solution)/shard_map/ppermute | solution.py:281
  11.9 0.7 %shard_map.49 = (f32[2,136,256]{2,1,0:T(8,128)S(1)}, f32[2,136,256]{2,1,0:T(8,128)S(1)}) custom-call(s32[1,3]{1,0:T(1,128)S(1)} %bitcast.4, bf16[256,256]{1,0:T(8,128)(2,1)S(1)} %copy-done, bf16[256,256]{1,0:T(8,128)(2,1)S(1)} %collective-permute-done.3.refs_2_.refs_1_, bf16[256,256]{1,0:T(8,128)(2,1)S(1)} %collective-permute-done.4.refs_3_, ...), custom_call_target="tpu_custom_call" | custom-call | flops 134217728 | tf_op jit(solution)/shard_map/pallas_call | solution.py:254
  12.6 0.0 collective-permute-done.2.refs_2_
  12.6 0.6 %shard_map.51 = bf16[2,144,256]{2,1,0:T(8,128)(2,1)S(1)} custom-call(s32[1,3]{1,0:T(1,128)S(1)} %bitcast.5, bf16[256,256]{1,0:T(8,128)(2,1)S(1)} %collective-permute-done.3.refs_2_.refs_1_, bf16[256,256]{1,0:T(8,128)(2,1)S(1)} %collective-permute-done.2.refs_2_, f32[2,136,256]{2,1,0:T(8,128)S(1)} %get-tuple-element.20.refs_3_), custom_call_target="tpu_custom_call" | custom-call | flops 67108864 | tf_op jit(solution)/shard_map/pallas_call | solution.py:254
  13.2 0.9 %collective-permute-start.7 = (bf16[2,144,256]{2,1,0:T(8,128)(2,1)S(1)}, bf16[2,144,256]{2,1,0:T(8,128)(2,1)S(1)}, u32[]{:S(2)}, u32[]{:S(2)}) collective-permute-start(bf16[2,144,256]{2,1,0:T(8,128)(2,1)S(1)} %shard_map.51), channel_id=1, source_target_pairs={{0,2},{2,0},{4,6},{6,4},{8,10},{10,8},{12,14},{14,12},{16,18},{18,... | collective-permute-start | bytes 442376 | tf_op jit(solution)/shard_map/ppermute | solution.py:306
  14.0 0.5 %shard_map.50.own_ref = f32[2,136,256]{2,1,0:T(8,128)S(1)} custom-call(s32[1,3]{1,0:T(1,128)S(1)} %bitcast.6, bf16[256,256]{1,0:T(8,128)(2,1)S(1)} %copy-done, bf16[256,256]{1,0:T(8,128)(2,1)S(1)} %collective-permute-done.2.refs_2_, f32[2,136,256]{2,1,0:T(8,128)S(1)} %get-tuple-element.19.refs_3_), custom_call_target="tpu_custom_call" | custom-call | flops 67108864 | tf_op jit(solution)/shard_map/pallas_call | solution.py:254
  14.6 0.5 %collective-permute-done.7.twin_ref = bf16[2,144,256]{2,1,0:T(8,128)(2,1)S(1)} collective-permute-done((bf16[2,144,256]{2,1,0:T(8,128)(2,1)S(1)}, bf16[2,144,256]{2,1,0:T(8,128)(2,1)S(1)}, u32[]{:S(2)}, u32[]{:S(2)}) %collective-permute-start.7) | collective-permute-done | bytes 147488 | tf_op jit(solution)/shard_map/ppermute | solution.py:306
  15.1 0.8 %shard_map.52 = bf16[256,256]{1,0:T(8,128)(2,1)} custom-call(f32[2,136,256]{2,1,0:T(8,128)S(1)} %shard_map.50.own_ref, bf16[2,144,256]{2,1,0:T(8,128)(2,1)S(1)} %collective-permute-done.7.twin_ref), custom_call_target="tpu_custom_call" | custom-call | flops 1000 | tf_op jit(solution)/shard_map/pallas_call | solution.py:254
  (5 shorter events, 0.1 us)
Async XLA Ops:
  0.0 3.1 %copy-start.2 = (bf16[256,128]{1,0:T(8,128)(2,1)S(1)}, bf16[256,128]{1,0:T(8,128)(2,1)}, u32[]{:S(2)}) copy-start(bf16[256,128]{1,0:T(8,128)(2,1)} %refs_4_.1) | copy-start | bytes 196612
  0.0 4.8 %copy-start = (bf16[256,256]{1,0:T(8,128)(2,1)S(1)}, bf16[256,256]{1,0:T(8,128)(2,1)}, u32[]{:S(2)}) copy-start(bf16[256,256]{1,0:T(8,128)(2,1)} %refs_1_.9) | copy-start | bytes 393220
  0.0 6.6 %collective-permute-start = (bf16[256,128]{1,0:T(8,128)(2,1)}, bf16[256,128]{1,0:T(8,128)(2,1)S(1)}, u32[]{:S(2)}, u32[]{:S(2)}) collective-permute-start(bf16[256,128]{1,0:T(8,128)(2,1)} %refs_3_.1), channel_id=1, source_target_pairs={{0,4},{2,6},{4,8},{6,10},{8,0},{10,2},{12,16},{14,18},{16,24},{18,... | collective-permute-start | bytes 196616 | tf_op jit(solution)/shard_map/ppermute | solution.py:281
  1.0 5.6 %collective-permute-start.1 = (bf16[256,128]{1,0:T(8,128)(2,1)}, bf16[256,128]{1,0:T(8,128)(2,1)S(1)}, u32[]{:S(2)}, u32[]{:S(2)}) collective-permute-start(bf16[256,128]{1,0:T(8,128)(2,1)} %refs_4_.1), channel_id=1, source_target_pairs={{0,4},{2,6},{4,8},{6,10},{8,0},{10,2},{12,16},{14,18},{16,24},{18,... | collective-permute-start | bytes 196616 | tf_op jit(solution)/shard_map/ppermute | solution.py:281
  3.1 5.7 %collective-permute-start.6 = (bf16[256,256]{1,0:T(8,128)(2,1)S(1)}, bf16[256,256]{1,0:T(8,128)(2,1)S(1)}, u32[]{:S(2)}, u32[]{:S(2)}) collective-permute-start(bf16[256,256]{1,0:T(8,128)(2,1)S(1)} %constant_dynamic-update-slice_fusion.2), channel_id=1, source_target_pairs={{0,8},{2,10},{4,6},{6,4},{8,0},{10,2},{12,28},{14,30},{16,20},{18,... | collective-permute-start | bytes 393224 | tf_op jit(solution)/shard_map/ppermute | solution.py:281
  4.4 5.0 %collective-permute-start.5 = (bf16[256,256]{1,0:T(8,128)(2,1)S(1)}, bf16[256,256]{1,0:T(8,128)(2,1)S(1)}, u32[]{:S(2)}, u32[]{:S(2)}) collective-permute-start(bf16[256,256]{1,0:T(8,128)(2,1)S(1)} %constant_dynamic-update-slice_fusion.2), channel_id=1, source_target_pairs={{0,2},{2,0},{4,6},{6,4},{8,10},{10,8},{12,20},{14,22},{16,18},{18,... | collective-permute-start | bytes 393224 | tf_op jit(solution)/shard_map/ppermute | solution.py:281
  4.8 2.8 %collective-permute-start.3 = (bf16[256,256]{1,0:T(8,128)(2,1)S(1)}, bf16[256,256]{1,0:T(8,128)(2,1)S(1)}, u32[]{:S(2)}, u32[]{:S(2)}) collective-permute-start(bf16[256,256]{1,0:T(8,128)(2,1)S(1)} %copy-done), channel_id=1, source_target_pairs={{0,2},{2,0},{4,6},{6,4},{8,10},{10,8},{12,14},{14,12},{16,18},{18,... | collective-permute-start | bytes 393224 | tf_op jit(solution)/shard_map/ppermute | solution.py:282
  6.6 1.0 %copy-start.1 = (bf16[256,128]{1,0:T(8,128)(2,1)S(1)}, bf16[256,128]{1,0:T(8,128)(2,1)}, u32[]{:S(2)}) copy-start(bf16[256,128]{1,0:T(8,128)(2,1)} %refs_3_.1) | copy-start | bytes 196612
  6.7 0.9 %copy-start.3 = (s32[3]{0:T(128)S(1)}, s32[3]{0:T(128)}, u32[]{:S(2)}) copy-start(s32[3]{0:T(128)} %param.7) | copy-start | bytes 40
  6.7 5.2 %collective-permute-start.4 = (bf16[256,256]{1,0:T(8,128)(2,1)S(1)}, bf16[256,256]{1,0:T(8,128)(2,1)S(1)}, u32[]{:S(2)}, u32[]{:S(2)}) collective-permute-start(bf16[256,256]{1,0:T(8,128)(2,1)S(1)} %constant_dynamic-update-slice_fusion), channel_id=1, source_target_pairs={{0,2},{2,0},{4,6},{6,4},{8,10},{10,8},{12,14},{14,12},{16,24},{18,... | collective-permute-start | bytes 393224 | tf_op jit(solution)/shard_map/ppermute | solution.py:281
  6.7 5.8 %collective-permute-start.2 = (bf16[256,256]{1,0:T(8,128)(2,1)S(1)}, bf16[256,256]{1,0:T(8,128)(2,1)S(1)}, u32[]{:S(2)}, u32[]{:S(2)}) collective-permute-start(bf16[256,256]{1,0:T(8,128)(2,1)S(1)} %constant_dynamic-update-slice_fusion), channel_id=1, source_target_pairs={{0,2},{2,0},{4,6},{6,4},{8,10},{10,8},{12,14},{14,12},{16,18},{18,... | collective-permute-start | bytes 393224 | tf_op jit(solution)/shard_map/ppermute | solution.py:281
  13.2 1.9 %collective-permute-start.7 = (bf16[2,144,256]{2,1,0:T(8,128)(2,1)S(1)}, bf16[2,144,256]{2,1,0:T(8,128)(2,1)S(1)}, u32[]{:S(2)}, u32[]{:S(2)}) collective-permute-start(bf16[2,144,256]{2,1,0:T(8,128)(2,1)S(1)} %shard_map.51), channel_id=1, source_target_pairs={{0,2},{2,0},{4,6},{6,4},{8,10},{10,8},{12,14},{14,12},{16,18},{18,... | collective-permute-start | bytes 442376 | tf_op jit(solution)/shard_map/ppermute | solution.py:306

commit v5 on v4

--- a/solution.py
+++ b/solution.py
@@ -207,7 +207,7 @@
         patterns = {tuple(edge <= table[chip] < chip for table in tables) for chip in range(edge, len(tables[0]))}
         joint = jnp.bool_(False)
         for pattern in sorted(patterns):
-            if sum(pattern) < 2:
+            if sum(pattern) < 1:
                 continue
             here = last_group
             for wanted, (_, _, useful, _) in zip(pattern, received):

time: 16 us -> 16 us (level)
  no operation moved by 1% of the time
where the time goes in v5:
time: 16 us; the launch traced here: 15.8 us
  starting transfers between devices  7.32 us (46%)
  Pallas kernels  3.9 us (24%)
  waiting for transfers between devices  3.53 us (22%)
  local copies, waits for them, and re-layouts  0.92 us (6%)
    ppermute x6, starting transfers between devices, shards(): lax.ppermute(part, 'ctx', over_cores(targets))  4.67 us
    pallas_call x7, Pallas kernels, vmem_call(): pl.pallas_call(kernel, out_shape=out_shape, in_specs=[vmem] * len(operand...  3.9 us
    ppermute x6, waiting for transfers between devices, shards(): lax.ppermute(part, 'ctx', over_cores(targets))  2.92 us
    ppermute x1, starting transfers between devices, shards(): both = (queries, lax.ppermute(queries, 'ctx', swap))  1.8 us
    unnamed x10, local copies, waits for them, and re-layouts  0.88 us
    ppermute x1, starting transfers between devices, shards(): lax.ppermute(others, 'ctx', swap)  0.86 us
    ppermute x1, waiting for transfers between devices, shards(): lax.ppermute(others, 'ctx', swap)  0.49 us
  transfers between devices with their start and end apart: 8, of which 4 were waited for; matrix products, arithmetic and copies ran while one was open for 6% of the time, Pallas kernels for 16%

profile of v5, /device:TPU:25, one launch (start us, length us, event | category | flops | bytes accessed | tf_op | source)
XLA Modules:
  0.0 15.8 jit_solution(5131275156599567798)
XLA Ops:
  0.0 0.0 copy-start.2
  0.0 0.0 copy-start
  0.0 1.0 %collective-permute-start = (bf16[256,128]{1,0:T(8,128)(2,1)}, bf16[256,128]{1,0:T(8,128)(2,1)S(1)}, u32[]{:S(2)}, u32[]{:S(2)}) collective-permute-start(bf16[256,128]{1,0:T(8,128)(2,1)} %refs_3_.1), channel_id=1, source_target_pairs={{0,4},{2,6},{4,8},{6,10},{8,0},{10,2},{12,16},{14,18},{16,24},{18,... | collective-permute-start | bytes 196616 | tf_op jit(solution)/shard_map/ppermute | solution.py:281
  1.0 1.3 %collective-permute-start.1 = (bf16[256,128]{1,0:T(8,128)(2,1)}, bf16[256,128]{1,0:T(8,128)(2,1)S(1)}, u32[]{:S(2)}, u32[]{:S(2)}) collective-permute-start(bf16[256,128]{1,0:T(8,128)(2,1)} %refs_4_.1), channel_id=1, source_target_pairs={{0,4},{2,6},{4,8},{6,10},{8,0},{10,2},{12,16},{14,18},{16,24},{18,... | collective-permute-start | bytes 196616 | tf_op jit(solution)/shard_map/ppermute | solution.py:281
  2.3 0.9 %constant_dynamic-update-slice_fusion.3 = bf16[256,256]{1,0:T(8,128)(2,1)S(1)} fusion(bf16[256,128]{1,0:T(8,128)(2,1)} %refs_3_.1), kind=kLoop, calls=%fused_computation.3 | loop fusion | bytes 131072
  3.1 0.0 copy-done.2
  3.1 1.3 %collective-permute-start.6 = (bf16[256,256]{1,0:T(8,128)(2,1)S(1)}, bf16[256,256]{1,0:T(8,128)(2,1)S(1)}, u32[]{:S(2)}, u32[]{:S(2)}) collective-permute-start(bf16[256,256]{1,0:T(8,128)(2,1)S(1)} %constant_dynamic-update-slice_fusion.2), channel_id=1, source_target_pairs={{0,8},{2,10},{4,6},{6,4},{8,0},{10,2},{12,28},{14,30},{16,20},{18,... | collective-permute-start | bytes 393224 | tf_op jit(solution)/shard_map/ppermute | solution.py:281
  4.4 0.3 %collective-permute-start.5 = (bf16[256,256]{1,0:T(8,128)(2,1)S(1)}, bf16[256,256]{1,0:T(8,128)(2,1)S(1)}, u32[]{:S(2)}, u32[]{:S(2)}) collective-permute-start(bf16[256,256]{1,0:T(8,128)(2,1)S(1)} %constant_dynamic-update-slice_fusion.2), channel_id=1, source_target_pairs={{0,2},{2,0},{4,6},{6,4},{8,10},{10,8},{12,20},{14,22},{16,18},{18,... | collective-permute-start | bytes 393224 | tf_op jit(solution)/shard_map/ppermute | solution.py:281
  4.8 0.0 copy-done
  4.8 1.8 %collective-permute-start.3 = (bf16[256,256]{1,0:T(8,128)(2,1)S(1)}, bf16[256,256]{1,0:T(8,128)(2,1)S(1)}, u32[]{:S(2)}, u32[]{:S(2)}) collective-permute-start(bf16[256,256]{1,0:T(8,128)(2,1)S(1)} %copy-done), channel_id=1, source_target_pairs={{0,2},{2,0},{4,6},{6,4},{8,10},{10,8},{12,14},{14,12},{16,18},{18,... | collective-permute-start | bytes 393224 | tf_op jit(solution)/shard_map/ppermute | solution.py:282
  6.6 0.0 collective-permute-done.refs_5_
  6.6 0.0 copy-start.1
  6.6 0.0 collective-permute-done.1.refs_6_
  6.7 0.0 copy-start.3
  6.7 0.1 collective-permute-start.4
  6.7 0.7 %collective-permute-start.2 = (bf16[256,256]{1,0:T(8,128)(2,1)S(1)}, bf16[256,256]{1,0:T(8,128)(2,1)S(1)}, u32[]{:S(2)}, u32[]{:S(2)}) collective-permute-start(bf16[256,256]{1,0:T(8,128)(2,1)S(1)} %constant_dynamic-update-slice_fusion), channel_id=1, source_target_pairs={{0,2},{2,0},{4,6},{6,4},{8,10},{10,8},{12,14},{14,12},{16,18},{18,... | collective-permute-start | bytes 393224 | tf_op jit(solution)/shard_map/ppermute | solution.py:281
  7.5 0.1 collective-permute-done.3.refs_2_.refs_1_
  7.6 0.0 copy-done.1
  7.6 0.0 copy-done.3
  7.6 1.2 %shard_map.46 = (f32[2,136,256]{2,1,0:T(8,128)S(1)}, f32[2,136,256]{2,1,0:T(8,128)S(1)}) custom-call(s32[1,3]{1,0:T(1,128)S(1)} %bitcast.1, bf16[256,256]{1,0:T(8,128)(2,1)S(1)} %copy-done, bf16[256,256]{1,0:T(8,128)(2,1)S(1)} %collective-permute-done.3.refs_2_.refs_1_, bf16[256,128]{1,0:T(8,128)(2,1)S(1)} %copy-done.1, bf16[256,128]{1,0:T(8,128)(2,1)S(1)} %copy-done.2, ...), custom_call_target="tpu_custom_call" | custom-call | flops 268435456 | tf_op jit(solution)/shard_map/pallas_call | solution.py:254
  8.8 0.0 collective-permute-done.6.refs_3_
  8.8 0.1 shard_map.47
  8.9 0.6 %collective-permute-done.5.refs_3_ = bf16[256,256]{1,0:T(8,128)(2,1)S(1)} collective-permute-done((bf16[256,256]{1,0:T(8,128)(2,1)S(1)}, bf16[256,256]{1,0:T(8,128)(2,1)S(1)}, u32[]{:S(2)}, u32[]{:S(2)}) %collective-permute-start.5) | collective-permute-done | bytes 131104 | tf_op jit(solution)/shard_map/ppermute | solution.py:281
  9.5 2.3 %collective-permute-done.4.refs_3_ = bf16[256,256]{1,0:T(8,128)(2,1)S(1)} collective-permute-done((bf16[256,256]{1,0:T(8,128)(2,1)S(1)}, bf16[256,256]{1,0:T(8,128)(2,1)S(1)}, u32[]{:S(2)}, u32[]{:S(2)}) %collective-permute-start.4) | collective-permute-done | bytes 131104 | tf_op jit(solution)/shard_map/ppermute | solution.py:281
  11.9 0.7 %shard_map.49 = (f32[2,136,256]{2,1,0:T(8,128)S(1)}, f32[2,136,256]{2,1,0:T(8,128)S(1)}) custom-call(s32[1,3]{1,0:T(1,128)S(1)} %bitcast.4, bf16[256,256]{1,0:T(8,128)(2,1)S(1)} %copy-done, bf16[256,256]{1,0:T(8,128)(2,1)S(1)} %collective-permute-done.3.refs_2_.refs_1_, bf16[256,256]{1,0:T(8,128)(2,1)S(1)} %collective-permute-done.4.refs_3_, ...), custom_call_target="tpu_custom_call" | custom-call | flops 134217728 | tf_op jit(solution)/shard_map/pallas_call | solution.py:254
  12.6 0.0 collective-permute-done.2.refs_2_
  12.6 0.6 %shard_map.51 = bf16[2,144,256]{2,1,0:T(8,128)(2,1)S(1)} custom-call(s32[1,3]{1,0:T(1,128)S(1)} %bitcast.5, bf16[256,256]{1,0:T(8,128)(2,1)S(1)} %collective-permute-done.3.refs_2_.refs_1_, bf16[256,256]{1,0:T(8,128)(2,1)S(1)} %collective-permute-done.2.refs_2_, f32[2,136,256]{2,1,0:T(8,128)S(1)} %get-tuple-element.20.refs_3_), custom_call_target="tpu_custom_call" | custom-call | flops 67108864 | tf_op jit(solution)/shard_map/pallas_call | solution.py:254
  13.1 0.9 %collective-permute-start.7 = (bf16[2,144,256]{2,1,0:T(8,128)(2,1)S(1)}, bf16[2,144,256]{2,1,0:T(8,128)(2,1)S(1)}, u32[]{:S(2)}, u32[]{:S(2)}) collective-permute-start(bf16[2,144,256]{2,1,0:T(8,128)(2,1)S(1)} %shard_map.51), channel_id=1, source_target_pairs={{0,2},{2,0},{4,6},{6,4},{8,10},{10,8},{12,14},{14,12},{16,18},{18,... | collective-permute-start | bytes 442376 | tf_op jit(solution)/shard_map/ppermute | solution.py:306
  14.0 0.5 %shard_map.50.own_ref = f32[2,136,256]{2,1,0:T(8,128)S(1)} custom-call(s32[1,3]{1,0:T(1,128)S(1)} %bitcast.6, bf16[256,256]{1,0:T(8,128)(2,1)S(1)} %copy-done, bf16[256,256]{1,0:T(8,128)(2,1)S(1)} %collective-permute-done.2.refs_2_, f32[2,136,256]{2,1,0:T(8,128)S(1)} %get-tuple-element.19.refs_3_), custom_call_target="tpu_custom_call" | custom-call | flops 67108864 | tf_op jit(solution)/shard_map/pallas_call | solution.py:254
  14.5 0.5 %collective-permute-done.7.twin_ref = bf16[2,144,256]{2,1,0:T(8,128)(2,1)S(1)} collective-permute-done((bf16[2,144,256]{2,1,0:T(8,128)(2,1)S(1)}, bf16[2,144,256]{2,1,0:T(8,128)(2,1)S(1)}, u32[]{:S(2)}, u32[]{:S(2)}) %collective-permute-start.7) | collective-permute-done | bytes 147488 | tf_op jit(solution)/shard_map/ppermute | solution.py:306
  15.0 0.8 %shard_map.52 = bf16[256,256]{1,0:T(8,128)(2,1)} custom-call(f32[2,136,256]{2,1,0:T(8,128)S(1)} %shard_map.50.own_ref, bf16[2,144,256]{2,1,0:T(8,128)(2,1)S(1)} %collective-permute-done.7.twin_ref), custom_call_target="tpu_custom_call" | custom-call | flops 1000 | tf_op jit(solution)/shard_map/pallas_call | solution.py:254
  (4 shorter events, 0.1 us)
Async XLA Ops:
  0.0 3.1 %copy-start.2 = (bf16[256,128]{1,0:T(8,128)(2,1)S(1)}, bf16[256,128]{1,0:T(8,128)(2,1)}, u32[]{:S(2)}) copy-start(bf16[256,128]{1,0:T(8,128)(2,1)} %refs_4_.1) | copy-start | bytes 196612
  0.0 4.8 %copy-start = (bf16[256,256]{1,0:T(8,128)(2,1)S(1)}, bf16[256,256]{1,0:T(8,128)(2,1)}, u32[]{:S(2)}) copy-start(bf16[256,256]{1,0:T(8,128)(2,1)} %refs_1_.9) | copy-start | bytes 393220
  0.0 6.6 %collective-permute-start = (bf16[256,128]{1,0:T(8,128)(2,1)}, bf16[256,128]{1,0:T(8,128)(2,1)S(1)}, u32[]{:S(2)}, u32[]{:S(2)}) collective-permute-start(bf16[256,128]{1,0:T(8,128)(2,1)} %refs_3_.1), channel_id=1, source_target_pairs={{0,4},{2,6},{4,8},{6,10},{8,0},{10,2},{12,16},{14,18},{16,24},{18,... | collective-permute-start | bytes 196616 | tf_op jit(solution)/shard_map/ppermute | solution.py:281
  1.0 5.6 %collective-permute-start.1 = (bf16[256,128]{1,0:T(8,128)(2,1)}, bf16[256,128]{1,0:T(8,128)(2,1)S(1)}, u32[]{:S(2)}, u32[]{:S(2)}) collective-permute-start(bf16[256,128]{1,0:T(8,128)(2,1)} %refs_4_.1), channel_id=1, source_target_pairs={{0,4},{2,6},{4,8},{6,10},{8,0},{10,2},{12,16},{14,18},{16,24},{18,... | collective-permute-start | bytes 196616 | tf_op jit(solution)/shard_map/ppermute | solution.py:281
  3.1 5.7 %collective-permute-start.6 = (bf16[256,256]{1,0:T(8,128)(2,1)S(1)}, bf16[256,256]{1,0:T(8,128)(2,1)S(1)}, u32[]{:S(2)}, u32[]{:S(2)}) collective-permute-start(bf16[256,256]{1,0:T(8,128)(2,1)S(1)} %constant_dynamic-update-slice_fusion.2), channel_id=1, source_target_pairs={{0,8},{2,10},{4,6},{6,4},{8,0},{10,2},{12,28},{14,30},{16,20},{18,... | collective-permute-start | bytes 393224 | tf_op jit(solution)/shard_map/ppermute | solution.py:281
  4.4 5.0 %collective-permute-start.5 = (bf16[256,256]{1,0:T(8,128)(2,1)S(1)}, bf16[256,256]{1,0:T(8,128)(2,1)S(1)}, u32[]{:S(2)}, u32[]{:S(2)}) collective-permute-start(bf16[256,256]{1,0:T(8,128)(2,1)S(1)} %constant_dynamic-update-slice_fusion.2), channel_id=1, source_target_pairs={{0,2},{2,0},{4,6},{6,4},{8,10},{10,8},{12,20},{14,22},{16,18},{18,... | collective-permute-start | bytes 393224 | tf_op jit(solution)/shard_map/ppermute | solution.py:281
  4.8 2.8 %collective-permute-start.3 = (bf16[256,256]{1,0:T(8,128)(2,1)S(1)}, bf16[256,256]{1,0:T(8,128)(2,1)S(1)}, u32[]{:S(2)}, u32[]{:S(2)}) collective-permute-start(bf16[256,256]{1,0:T(8,128)(2,1)S(1)} %copy-done), channel_id=1, source_target_pairs={{0,2},{2,0},{4,6},{6,4},{8,10},{10,8},{12,14},{14,12},{16,18},{18,... | collective-permute-start | bytes 393224 | tf_op jit(solution)/shard_map/ppermute | solution.py:282
  6.6 1.0 %copy-start.1 = (bf16[256,128]{1,0:T(8,128)(2,1)S(1)}, bf16[256,128]{1,0:T(8,128)(2,1)}, u32[]{:S(2)}) copy-start(bf16[256,128]{1,0:T(8,128)(2,1)} %refs_3_.1) | copy-start | bytes 196612
  6.7 0.9 %copy-start.3 = (s32[3]{0:T(128)S(1)}, s32[3]{0:T(128)}, u32[]{:S(2)}) copy-start(s32[3]{0:T(128)} %param.7) | copy-start | bytes 40
  6.7 5.2 %collective-permute-start.4 = (bf16[256,256]{1,0:T(8,128)(2,1)S(1)}, bf16[256,256]{1,0:T(8,128)(2,1)S(1)}, u32[]{:S(2)}, u32[]{:S(2)}) collective-permute-start(bf16[256,256]{1,0:T(8,128)(2,1)S(1)} %constant_dynamic-update-slice_fusion), channel_id=1, source_target_pairs={{0,2},{2,0},{4,6},{6,4},{8,10},{10,8},{12,14},{14,12},{16,24},{18,... | collective-permute-start | bytes 393224 | tf_op jit(solution)/shard_map/ppermute | solution.py:281
  6.7 5.8 %collective-permute-start.2 = (bf16[256,256]{1,0:T(8,128)(2,1)S(1)}, bf16[256,256]{1,0:T(8,128)(2,1)S(1)}, u32[]{:S(2)}, u32[]{:S(2)}) collective-permute-start(bf16[256,256]{1,0:T(8,128)(2,1)S(1)} %constant_dynamic-update-slice_fusion), channel_id=1, source_target_pairs={{0,2},{2,0},{4,6},{6,4},{8,10},{10,8},{12,14},{14,12},{16,18},{18,... | collective-permute-start | bytes 393224 | tf_op jit(solution)/shard_map/ppermute | solution.py:281
  13.1 1.9 %collective-permute-start.7 = (bf16[2,144,256]{2,1,0:T(8,128)(2,1)S(1)}, bf16[2,144,256]{2,1,0:T(8,128)(2,1)S(1)}, u32[]{:S(2)}, u32[]{:S(2)}) collective-permute-start(bf16[2,144,256]{2,1,0:T(8,128)(2,1)S(1)} %shard_map.51), channel_id=1, source_target_pairs={{0,2},{2,0},{4,6},{6,4},{8,10},{10,8},{12,14},{14,12},{16,18},{18,... | collective-permute-start | bytes 442376 | tf_op jit(solution)/shard_map/ppermute | solution.py:306

commit v6 on v5

--- a/solution.py
+++ b/solution.py
@@ -47,18 +47,17 @@
 def slots_of(chips):
     if chips == 8:
         return [
-            (None, True, [1, 2, 0, 4, 6, 7, 3, 5], None),
-            (None, False, [2, None, 0, 7, 5, 4, None, 3], None),
-            (None, False, [None, None, None, 5, None, 3, 7, 6], None),
-            (0, False, [None, None, None, None, None, None, 7, 6], None),
-            (0, False, [None, None, None, None, 6, None, 4, None], None),
+            (None, False, [1, 2, 0, 4, 6, 7, 3, 5], None),
+            (None, False, [2, None, 0, 6, 5, 4, 7, 3], None),
+            (None, False, [None, None, None, 7, None, None, None, 3], None),
+            (0, False, [None, None, None, None, 5, 4, 7, 6], None),
         ]
     return rotations(chips)
 
 
 def stages_of(chips, count):
     if chips == 8:
-        return [[0], [1], [2], [4], [3]]
+        return [[0], [1], [2, 3]]
     return [list(range(low, min(low + 4, count))) for low in range(0, count, 4)]
 
 

time: 16 us -> 16 us (level)
  waiting for transfers between devices: 3.53 us -> 6.65 us
  starting transfers between devices: 7.32 us -> 4.45 us
    ppermute x6 -> x4, waiting for transfers between devices: 2.92 us -> 6.17 us  [shards(): lax.ppermute(part, 'ctx', over_cores(targets))]
    ppermute x6 -> x4, starting transfers between devices: 4.67 us -> 2.93 us  [shards(): lax.ppermute(part, 'ctx', over_cores(targets))]
    ppermute x1, starting transfers between devices: 1.8 us -> 0.96 us  [shards(): both = (queries, lax.ppermute(queries, 'ctx', swap))]
    ppermute x1, starting transfers between devices: 0.86 us -> 0.57 us  [shards(): lax.ppermute(others, 'ctx', swap)]
    pallas_call x7 -> x5, Pallas kernels: 3.9 us -> 3.8 us  [vmem_call(): pl.pallas_call(kernel, out_shape=out_shape, in_specs=[vmem] * len(operand...]
    unnamed x10 -> x7, local copies, waits for them, and re-layouts: 0.88 us -> 0.9 us
  transfers between devices with their start and end apart: 8 -> 6, of which waited for: 4 -> 4; matrix products, arithmetic and copies ran while one was open for 6% -> 0% of each run, Pallas kernels for 16% -> 15%
where the time goes in v6:
time: 16 us; the launch traced here: 15.9 us
  waiting for transfers between devices  6.65 us (42%)
  starting transfers between devices  4.45 us (28%)
  Pallas kernels  3.8 us (24%)
  local copies, waits for them, and re-layouts  0.92 us (6%)
    ppermute x4, waiting for transfers between devices, shards(): lax.ppermute(part, 'ctx', over_cores(targets))  6.17 us
    pallas_call x5, Pallas kernels, vmem_call(): pl.pallas_call(kernel, out_shape=out_shape, in_specs=[vmem] * len(operand...  3.8 us
    ppermute x4, starting transfers between devices, shards(): lax.ppermute(part, 'ctx', over_cores(targets))  2.93 us
    ppermute x1, starting transfers between devices, shards(): both = (queries, lax.ppermute(queries, 'ctx', swap))  0.96 us
    unnamed x7, local copies, waits for them, and re-layouts  0.9 us
    ppermute x1, starting transfers between devices, shards(): lax.ppermute(others, 'ctx', swap)  0.57 us
    ppermute x1, waiting for transfers between devices, shards(): lax.ppermute(others, 'ctx', swap)  0.48 us
  transfers between devices with their start and end apart: 6, of which 4 were waited for; matrix products, arithmetic and copies ran while one was open for 0% of the time, Pallas kernels for 15%

profile of v6, /device:TPU:25, one launch (start us, length us, event | category | flops | bytes accessed | tf_op | source)
XLA Modules:
  0.0 15.9 jit_solution(6301237567613765864)
XLA Ops:
  0.0 0.0 copy-start.2
  0.0 0.0 copy-start
  0.0 0.9 %constant_dynamic-update-slice_fusion.1 = bf16[256,256]{1,0:T(8,128)(2,1)S(1)} fusion(bf16[256,128]{1,0:T(8,128)(2,1)} %param.5), kind=kLoop, calls=%fused_computation.1 | loop fusion | bytes 131072
  0.9 0.0 copy-done.2
  0.9 0.0 copy-start.1
  0.9 1.0 %collective-permute-start.1 = (bf16[256,256]{1,0:T(8,128)(2,1)S(1)}, bf16[256,256]{1,0:T(8,128)(2,1)S(1)}, u32[]{:S(2)}, u32[]{:S(2)}) collective-permute-start(bf16[256,256]{1,0:T(8,128)(2,1)S(1)} %constant_dynamic-update-slice_fusion.refs_3_), channel_id=1, source_target_pairs={{0,4},{2,6},{4,8},{6,10},{8,0},{10,2},{12,16},{14,18},{16,24},{18,... | collective-permute-start | bytes 393224 | tf_op jit(solution)/shard_map/ppermute | solution.py:280
  2.0 0.0 copy-done
  2.0 1.0 %collective-permute-start.3 = (bf16[256,256]{1,0:T(8,128)(2,1)S(1)}, bf16[256,256]{1,0:T(8,128)(2,1)S(1)}, u32[]{:S(2)}, u32[]{:S(2)}) collective-permute-start(bf16[256,256]{1,0:T(8,128)(2,1)S(1)} %copy-done), channel_id=1, source_target_pairs={{0,2},{2,0},{4,6},{6,4},{8,10},{10,8},{12,14},{14,12},{16,18},{18,... | collective-permute-start | bytes 393224 | tf_op jit(solution)/shard_map/ppermute | solution.py:281
  2.9 0.4 %collective-permute-start.4 = (bf16[256,256]{1,0:T(8,128)(2,1)S(1)}, bf16[256,256]{1,0:T(8,128)(2,1)S(1)}, u32[]{:S(2)}, u32[]{:S(2)}) collective-permute-start(bf16[256,256]{1,0:T(8,128)(2,1)S(1)} %constant_dynamic-update-slice_fusion.refs_3_), channel_id=1, source_target_pairs={{0,8},{2,10},{4,6},{6,4},{8,0},{10,2},{12,24},{14,26},{16,20},{18,... | collective-permute-start | bytes 393224 | tf_op jit(solution)/shard_map/ppermute | solution.py:280
  3.3 0.3 %collective-permute-start = (bf16[256,256]{1,0:T(8,128)(2,1)S(1)}, bf16[256,256]{1,0:T(8,128)(2,1)S(1)}, u32[]{:S(2)}, u32[]{:S(2)}) collective-permute-start(bf16[256,256]{1,0:T(8,128)(2,1)S(1)} %constant_dynamic-update-slice_fusion.refs_3_), channel_id=1, source_target_pairs={{0,2},{2,0},{4,6},{6,4},{8,10},{10,8},{12,28},{14,30},{16,18},{18,... | collective-permute-start | bytes 393224 | tf_op jit(solution)/shard_map/ppermute | solution.py:280
  3.6 1.7 %collective-permute-done.1.refs_4_ = bf16[256,256]{1,0:T(8,128)(2,1)S(1)} collective-permute-done((bf16[256,256]{1,0:T(8,128)(2,1)S(1)}, bf16[256,256]{1,0:T(8,128)(2,1)S(1)}, u32[]{:S(2)}, u32[]{:S(2)}) %collective-permute-start.1) | collective-permute-done | bytes 131104 | tf_op jit(solution)/shard_map/ppermute | solution.py:280
  5.4 1.2 %collective-permute-start.2 = (bf16[256,256]{1,0:T(8,128)(2,1)S(1)}, bf16[256,256]{1,0:T(8,128)(2,1)S(1)}, u32[]{:S(2)}, u32[]{:S(2)}) collective-permute-start(bf16[256,256]{1,0:T(8,128)(2,1)S(1)} %collective-permute-done.1.refs_4_), channel_id=1, source_target_pairs={{0,2},{2,0},{4,6},{6,4},{8,10},{10,8},{12,14},{14,12},{16,20},{18,... | collective-permute-start | bytes 393224 | tf_op jit(solution)/shard_map/ppermute | solution.py:280
  6.6 0.0 collective-permute-done.3.refs_2_.refs_1_
  6.6 0.0 copy-done.1
  6.6 1.2 %shard_map.46 = (f32[2,136,256]{2,1,0:T(8,128)S(1)}, f32[2,136,256]{2,1,0:T(8,128)S(1)}) custom-call(s32[1,3]{1,0:T(1,128)S(1)} %bitcast.1, bf16[256,256]{1,0:T(8,128)(2,1)S(1)} %copy-done, bf16[256,256]{1,0:T(8,128)(2,1)S(1)} %collective-permute-done.3.refs_2_.refs_1_, bf16[256,256]{1,0:T(8,128)(2,1)S(1)} %constant_dynamic-update-slice_fusion.refs_3_, ...), custom_call_target="tpu_custom_call" | custom-call | flops 268435456 | tf_op jit(solution)/shard_map/pallas_call | solution.py:253
  7.8 2.1 %collective-permute-done.4.refs_3_ = bf16[256,256]{1,0:T(8,128)(2,1)S(1)} collective-permute-done((bf16[256,256]{1,0:T(8,128)(2,1)S(1)}, bf16[256,256]{1,0:T(8,128)(2,1)S(1)}, u32[]{:S(2)}, u32[]{:S(2)}) %collective-permute-start.4) | collective-permute-done | bytes 131104 | tf_op jit(solution)/shard_map/ppermute | solution.py:280
  9.9 0.7 %shard_map.47 = (f32[2,136,256]{2,1,0:T(8,128)S(1)}, f32[2,136,256]{2,1,0:T(8,128)S(1)}) custom-call(s32[1,3]{1,0:T(1,128)S(1)} %bitcast.2, bf16[256,256]{1,0:T(8,128)(2,1)S(1)} %copy-done, bf16[256,256]{1,0:T(8,128)(2,1)S(1)} %collective-permute-done.3.refs_2_.refs_1_, bf16[256,256]{1,0:T(8,128)(2,1)S(1)} %collective-permute-done.4.refs_3_, ...), custom_call_target="tpu_custom_call" | custom-call | flops 134217728 | tf_op jit(solution)/shard_map/pallas_call | solution.py:253
  10.6 0.0 collective-permute-done.refs_2_
  10.6 2.4 %collective-permute-done.2.refs_3_ = bf16[256,256]{1,0:T(8,128)(2,1)S(1)} collective-permute-done((bf16[256,256]{1,0:T(8,128)(2,1)S(1)}, bf16[256,256]{1,0:T(8,128)(2,1)S(1)}, u32[]{:S(2)}, u32[]{:S(2)}) %collective-permute-start.2) | collective-permute-done | bytes 131104 | tf_op jit(solution)/shard_map/ppermute | solution.py:280
  12.9 0.6 %shard_map.49 = bf16[2,144,256]{2,1,0:T(8,128)(2,1)S(1)} custom-call(s32[1,3]{1,0:T(1,128)S(1)} %bitcast.3, bf16[256,256]{1,0:T(8,128)(2,1)S(1)} %collective-permute-done.3.refs_2_.refs_1_, bf16[256,256]{1,0:T(8,128)(2,1)S(1)} %collective-permute-done.refs_2_, bf16[256,256]{1,0:T(8,128)(2,1)S(1)} %collective-permute-done.2.refs_3_, ...), custom_call_target="tpu_custom_call" | custom-call | flops 134217728 | tf_op jit(solution)/shard_map/pallas_call | solution.py:253
  13.5 0.6 %collective-permute-start.5 = (bf16[2,144,256]{2,1,0:T(8,128)(2,1)S(1)}, bf16[2,144,256]{2,1,0:T(8,128)(2,1)S(1)}, u32[]{:S(2)}, u32[]{:S(2)}) collective-permute-start(bf16[2,144,256]{2,1,0:T(8,128)(2,1)S(1)} %shard_map.49), channel_id=1, source_target_pairs={{0,2},{2,0},{4,6},{6,4},{8,10},{10,8},{12,14},{14,12},{16,18},{18,... | collective-permute-start | bytes 442376 | tf_op jit(solution)/shard_map/ppermute | solution.py:305
  14.1 0.5 %shard_map.48.own_ref = f32[2,136,256]{2,1,0:T(8,128)S(1)} custom-call(s32[1,3]{1,0:T(1,128)S(1)} %bitcast.4, bf16[256,256]{1,0:T(8,128)(2,1)S(1)} %copy-done, bf16[256,256]{1,0:T(8,128)(2,1)S(1)} %collective-permute-done.refs_2_, bf16[256,256]{1,0:T(8,128)(2,1)S(1)} %collective-permute-done.2.refs_3_, f32[2,136,256]{2,1,0:T(8,128)S(1)} %get-tuple-element.11.refs_4_), custom_call_target="tpu_custom_call" | custom-call | flops 134217728 | tf_op jit(solution)/shard_map/pallas_call | solution.py:253
  14.6 0.5 %collective-permute-done.5.twin_ref = bf16[2,144,256]{2,1,0:T(8,128)(2,1)S(1)} collective-permute-done((bf16[2,144,256]{2,1,0:T(8,128)(2,1)S(1)}, bf16[2,144,256]{2,1,0:T(8,128)(2,1)S(1)}, u32[]{:S(2)}, u32[]{:S(2)}) %collective-permute-start.5) | collective-permute-done | bytes 147488 | tf_op jit(solution)/shard_map/ppermute | solution.py:305
  15.1 0.8 %shard_map.50 = bf16[256,256]{1,0:T(8,128)(2,1)} custom-call(f32[2,136,256]{2,1,0:T(8,128)S(1)} %shard_map.48.own_ref, bf16[2,144,256]{2,1,0:T(8,128)(2,1)S(1)} %collective-permute-done.5.twin_ref), custom_call_target="tpu_custom_call" | custom-call | flops 1000 | tf_op jit(solution)/shard_map/pallas_call | solution.py:253
  (1 shorter events, 0.0 us)
Async XLA Ops:
  0.0 0.9 %copy-start.2 = (bf16[256,128]{1,0:T(8,128)(2,1)S(1)}, bf16[256,128]{1,0:T(8,128)(2,1)}, u32[]{:S(2)}) copy-start(bf16[256,128]{1,0:T(8,128)(2,1)} %param.6) | copy-start | bytes 196612
  0.0 2.0 %copy-start = (bf16[256,256]{1,0:T(8,128)(2,1)S(1)}, bf16[256,256]{1,0:T(8,128)(2,1)}, u32[]{:S(2)}) copy-start(bf16[256,256]{1,0:T(8,128)(2,1)} %refs_1_.5) | copy-start | bytes 393220
  0.9 5.6 %copy-start.1 = (s32[3]{0:T(128)S(1)}, s32[3]{0:T(128)}, u32[]{:S(2)}) copy-start(s32[3]{0:T(128)} %param.7) | copy-start | bytes 40
  0.9 4.4 %collective-permute-start.1 = (bf16[256,256]{1,0:T(8,128)(2,1)S(1)}, bf16[256,256]{1,0:T(8,128)(2,1)S(1)}, u32[]{:S(2)}, u32[]{:S(2)}) collective-permute-start(bf16[256,256]{1,0:T(8,128)(2,1)S(1)} %constant_dynamic-update-slice_fusion.refs_3_), channel_id=1, source_target_pairs={{0,4},{2,6},{4,8},{6,10},{8,0},{10,2},{12,16},{14,18},{16,24},{18,... | collective-permute-start | bytes 393224 | tf_op jit(solution)/shard_map/ppermute | solution.py:280
  2.0 4.6 %collective-permute-start.3 = (bf16[256,256]{1,0:T(8,128)(2,1)S(1)}, bf16[256,256]{1,0:T(8,128)(2,1)S(1)}, u32[]{:S(2)}, u32[]{:S(2)}) collective-permute-start(bf16[256,256]{1,0:T(8,128)(2,1)S(1)} %copy-done), channel_id=1, source_target_pairs={{0,2},{2,0},{4,6},{6,4},{8,10},{10,8},{12,14},{14,12},{16,18},{18,... | collective-permute-start | bytes 393224 | tf_op jit(solution)/shard_map/ppermute | solution.py:281
  2.9 6.9 %collective-permute-start.4 = (bf16[256,256]{1,0:T(8,128)(2,1)S(1)}, bf16[256,256]{1,0:T(8,128)(2,1)S(1)}, u32[]{:S(2)}, u32[]{:S(2)}) collective-permute-start(bf16[256,256]{1,0:T(8,128)(2,1)S(1)} %constant_dynamic-update-slice_fusion.refs_3_), channel_id=1, source_target_pairs={{0,8},{2,10},{4,6},{6,4},{8,0},{10,2},{12,24},{14,26},{16,20},{18,... | collective-permute-start | bytes 393224 | tf_op jit(solution)/shard_map/ppermute | solution.py:280
  3.3 7.2 %collective-permute-start = (bf16[256,256]{1,0:T(8,128)(2,1)S(1)}, bf16[256,256]{1,0:T(8,128)(2,1)S(1)}, u32[]{:S(2)}, u32[]{:S(2)}) collective-permute-start(bf16[256,256]{1,0:T(8,128)(2,1)S(1)} %constant_dynamic-update-slice_fusion.refs_3_), channel_id=1, source_target_pairs={{0,2},{2,0},{4,6},{6,4},{8,10},{10,8},{12,28},{14,30},{16,18},{18,... | collective-permute-start | bytes 393224 | tf_op jit(solution)/shard_map/ppermute | solution.py:280
  5.4 7.6 %collective-permute-start.2 = (bf16[256,256]{1,0:T(8,128)(2,1)S(1)}, bf16[256,256]{1,0:T(8,128)(2,1)S(1)}, u32[]{:S(2)}, u32[]{:S(2)}) collective-permute-start(bf16[256,256]{1,0:T(8,128)(2,1)S(1)} %collective-permute-done.1.refs_4_), channel_id=1, source_target_pairs={{0,2},{2,0},{4,6},{6,4},{8,10},{10,8},{12,14},{14,12},{16,20},{18,... | collective-permute-start | bytes 393224 | tf_op jit(solution)/shard_map/ppermute | solution.py:280
  13.5 1.6 %collective-permute-start.5 = (bf16[2,144,256]{2,1,0:T(8,128)(2,1)S(1)}, bf16[2,144,256]{2,1,0:T(8,128)(2,1)S(1)}, u32[]{:S(2)}, u32[]{:S(2)}) collective-permute-start(bf16[2,144,256]{2,1,0:T(8,128)(2,1)S(1)} %shard_map.49), channel_id=1, source_target_pairs={{0,2},{2,0},{4,6},{6,4},{8,10},{10,8},{12,14},{14,12},{16,18},{18,... | collective-permute-start | bytes 442376 | tf_op jit(solution)/shard_map/ppermute | solution.py:305
